TPU v7x, 256 devices: a whole 4x4x8 slice. The times are simulated.
256 devices in a mesh: seq: 32 (over y, z), head: 8 (over x, core).
Axes of the slice: x: 4, y: 4, z: 8, core: 2. Of those that a mesh axis runs over, the one named last changes fastest.
Arguments:
- queries: bfloat16 [131072, 8, 256], P('seq', 'head'), may hold values from -6 to 6
- key_vectors: bfloat16 [131072, 8, 256], P('seq', 'head'), may hold values from -6 to 6
- value_vectors: bfloat16 [131072, 8, 512], P('seq', 'head'), may hold values from -21 to 21
- input_gate: float32 [8, 131072], P('head', 'seq'), may hold values from -90 to 150, as said below
- forget_gate: float32 [8, 131072], P('head', 'seq'), may hold values from -0.01 to 20, as said below
- norm_gain: float32 [4096], replicated, may hold values from 0.1 to 1.9
Outputs:
- cell_output: bfloat16 [131072, 4096], P(('seq', 'head'))
Inputs may be any that keep to these rules, and one draw needn't show every extreme that they name: `input_gate`: input gate preactivations of every head and token. `forget_gate`: forget gate preactivations of every head and token.
All inputs are finite; a program needn't handle non-finite values.
Results may differ from a plain program's by a relative error of at most 0.02.
Values may be sent and summed in bfloat16 or wider, within the bound.
No kernel may reach another device: no remote copies, remote signals or barrier semaphores. Data moves between devices by JAX's collectives and lax.ppermute only.
A program may use at most 128 MiB of HBM per device.

v0:
```python
import math

import jax
import jax.numpy as jnp
from jax import lax
from jax.sharding import PartitionSpec as P

CH = 64


FLOOR_LOG = -1e30
EPSILON = 1e-06


def entering(value, axis, join, neutral):
    count, mine = (lax.axis_size(axis), lax.axis_index(axis))
    pieces = jax.tree.map(lambda part: lax.all_gather(part, axis), value)
    total = jax.tree.map(
        lambda part, zero: jnp.full_like(part, 0) + jnp.asarray(zero, part.dtype), value, neutral
    )

    def hop(position, total):
        longer = join(total, jax.tree.map(lambda part: part[position], pieces))
        return jax.tree.map(lambda new, old: jnp.where(position < mine, new, old), longer, total)

    return lax.fori_loop(0, count - 1, hop, total)


def split_pair(state):
    high = lax.optimization_barrier(state.astype(jnp.bfloat16))
    low = (state - high.astype(jnp.float32)).astype(jnp.bfloat16)
    return (high, low)


def combine_states(earlier, later):
    early_matrix, early_vector, early_level, early_decay = earlier
    late_matrix, late_vector, late_level, late_decay = later
    shifted = early_level + late_decay
    new_level = jnp.maximum(shifted, late_level)
    old_scale = jnp.exp(shifted - new_level)
    new_scale = jnp.exp(late_level - new_level)
    return (
        old_scale[..., None, None] * early_matrix + new_scale[..., None, None] * late_matrix,
        old_scale[..., None] * early_vector + new_scale[..., None] * late_vector,
        new_level,
        early_decay + late_decay,
    )


def block_states(key_block, value_block, input_block, decay_block):
    within = jnp.cumsum(decay_block, axis=-1)
    block_total = within[..., -1]
    key_log = block_total[..., None] - within + input_block
    key_top = jnp.max(key_log, axis=-1)
    key_weight = jnp.transpose(jnp.exp(key_log - key_top[..., None]), (1, 2, 0))
    weighted = (key_block * key_weight[..., None]).astype(jnp.bfloat16)
    block_matrix = jnp.einsum(
        "csjk,csjv->jckv", weighted, value_block, preferred_element_type=jnp.float32
    )
    block_vector = jnp.transpose(jnp.sum(weighted.astype(jnp.float32), axis=1), (1, 0, 2))
    return (within, block_total, key_top, block_matrix, block_vector)


def fold_blocks(carried, block_parts):
    within, block_total, key_top, block_matrix, block_vector = block_parts
    start_matrix, start_vector, start_level = ([], [], [])
    for number in range(block_matrix.shape[1]):
        start_matrix.append(carried[0])
        start_vector.append(carried[1])
        start_level.append(carried[2])
        carried = combine_states(
            carried,
            (
                block_matrix[:, number],
                block_vector[:, number],
                key_top[:, number],
                block_total[:, number],
            ),
        )
    starts = (jnp.stack(start_matrix, 1), jnp.stack(start_vector, 1), jnp.stack(start_level, 1))
    return (starts, carried)


def advance_states(carried, inputs):
    key_block, value_block, input_block, decay_block = inputs
    starts, carried = fold_blocks(
        carried, block_states(key_block, value_block, input_block, decay_block)
    )
    return (carried, None)


def block_terms(carried, inputs):
    query_block, key_block, value_block, input_block, decay_block = inputs
    block_parts = block_states(key_block, value_block, input_block, decay_block)
    within = block_parts[0]
    starts, carried = fold_blocks(carried, block_parts)
    start_matrix, start_vector, start_level = starts
    qk_scale = 1.0 / math.sqrt(query_block.shape[-1])
    width_rows = within.shape[-1]
    causal = jnp.arange(width_rows)[:, None] >= jnp.arange(width_rows)[None, :]
    scores = (
        jnp.einsum("ctjk,csjk->jcts", query_block, key_block, preferred_element_type=jnp.float32)
        * qk_scale
    )
    pair_log = jnp.where(
        causal, within[..., :, None] - within[..., None, :] + input_block[..., None, :], -jnp.inf
    )
    pair_top = jnp.max(pair_log, axis=-1)
    pair_probs = jnp.exp(pair_log - pair_top[..., None]) * scores
    intra_numer = jnp.einsum(
        "jcts,csjv->ctjv",
        pair_probs.astype(jnp.bfloat16),
        value_block,
        preferred_element_type=jnp.float32,
    )
    intra_denom = jnp.transpose(jnp.sum(pair_probs, axis=-1), (1, 2, 0))
    matrix_high, matrix_low = split_pair(start_matrix)
    vector_high, vector_low = split_pair(start_vector)
    carry_numer = (
        jnp.einsum("ctjk,jckv->ctjv", query_block, matrix_high, preferred_element_type=jnp.float32)
        + jnp.einsum("ctjk,jckv->ctjv", query_block, matrix_low, preferred_element_type=jnp.float32)
    ) * qk_scale
    carry_denom = (
        jnp.einsum("ctjk,jck->ctj", query_block, vector_high, preferred_element_type=jnp.float32)
        + jnp.einsum("ctjk,jck->ctj", query_block, vector_low, preferred_element_type=jnp.float32)
    ) * qk_scale
    pair_level = jnp.transpose(pair_top, (1, 2, 0))
    carry_log = jnp.transpose(within + start_level[..., None], (1, 2, 0))
    row_level = jnp.maximum(pair_level, carry_log)
    own_scale = jnp.exp(pair_level - row_level)
    far_scale = jnp.exp(carry_log - row_level)
    numerator = own_scale[..., None] * intra_numer + far_scale[..., None] * carry_numer
    denominator = own_scale * intra_denom + far_scale * carry_denom
    return (carried, (numerator, denominator, row_level))


def carried_in(aggregate, empty_state):
    agg_matrix, agg_vector, agg_level, agg_decay = aggregate
    before = entering(
        (agg_matrix, agg_vector, agg_level, agg_decay),
        "seq",
        combine_states,
        (empty_state[0], empty_state[1], empty_state[2], empty_state[3]),
    )
    result = (before[0], before[1], before[2])
    return result


def shards(queries, key_vectors, value_vectors, input_gate, forget_gate, norm_gain):
    tok_rows, heads_here, key_width = queries.shape
    value_width = value_vectors.shape[2]
    span_rows = min(512, tok_rows)
    block_count = tok_rows // span_rows
    per_block = span_rows // CH
    log_gate = jax.nn.log_sigmoid(forget_gate)

    def split_rows(array):
        return array.reshape((block_count, per_block, CH) + array.shape[1:])

    def split_gate(array):
        return jnp.transpose(array.reshape(heads_here, block_count, per_block, CH), (1, 0, 2, 3))

    query_blocks = split_rows(queries)
    key_blocks = split_rows(key_vectors)
    value_blocks = split_rows(value_vectors)
    input_blocks = split_gate(input_gate)
    decay_blocks = split_gate(log_gate)
    zero_decay = jnp.zeros((heads_here,), jnp.float32)
    empty_state = (
        jnp.zeros((heads_here, key_width, value_width), jnp.float32),
        jnp.zeros((heads_here, key_width), jnp.float32),
        jnp.full((heads_here,), FLOOR_LOG, jnp.float32),
        zero_decay,
    )
    feeds = (query_blocks, key_blocks, value_blocks, input_blocks, decay_blocks)
    aggregate, unused = lax.scan(
        advance_states, empty_state, (key_blocks, value_blocks, input_blocks, decay_blocks)
    )
    in_matrix, in_vector, in_level = carried_in(aggregate, empty_state)
    finished, outputs = lax.scan(block_terms, (in_matrix, in_vector, in_level, zero_decay), feeds)
    numerator = outputs[0].reshape(tok_rows, heads_here, value_width)
    denominator = outputs[1].reshape(tok_rows, heads_here)
    hidden = (numerator / jnp.maximum(jnp.abs(denominator), 1.0)[..., None]).astype(jnp.bfloat16)
    owners = lax.axis_size("head")
    grouped = hidden.reshape(owners, tok_rows // owners, heads_here * value_width)
    wide = lax.all_to_all(grouped, "head", split_axis=0, concat_axis=2, tiled=True).astype(
        jnp.float32
    )
    factor = lax.rsqrt(jnp.mean(wide * wide, axis=-1, keepdims=True) + EPSILON)
    mixed = (wide * factor * norm_gain).astype(jnp.bfloat16)
    return mixed.reshape(mixed.shape[1], mixed.shape[2])


def solution(mesh):
    in_specs = (
        P("seq", "head", None),
        P("seq", "head", None),
        P("seq", "head", None),
        P("head", "seq"),
        P("head", "seq"),
        P(),
    )
    out_specs = P(("seq", "head"), None)
    return jax.shard_map(shards, mesh=mesh, in_specs=in_specs, out_specs=out_specs, check_vma=False)
```

profile of v0, /device:TPU:1, one launch (start us, length us, event | category | flops | bytes accessed | tf_op | source)
XLA Modules:
  0.0 943.8 jit_solution(12861833787392829957)
XLA Ops:
  9.4 245.9 %while.54 = (s32[]{:T(128)}, f32[1,256,512]{2,1,0:T(8,128)S(1)}, f32[1,256]{1,0:T(1,128)S(1)}, f32[1]{0:T(128)}, f32[1]{0:T(128)}, /*index=5*/f32[8,1,8,64]{3,2,...) while((s32[]{:T(128)}, f32[1,256,512]{2,1,0:T(8,128)S(1)}, ...), condition=%wide.region_4.5_spmd.clone, body=%wide.region_0.4_spmd.clone.sunk | while | flops 138582784 | bytes 10528956 | solution.py:176
  10.1 4.3 convolution_bitcast_fusion.6
  31.3 2.7 fusion.224
  40.8 4.3 convolution_bitcast_fusion.6
  62.0 2.7 fusion.224
  71.6 4.3 convolution_bitcast_fusion.6
  92.7 2.7 fusion.224
  102.3 4.3 convolution_bitcast_fusion.6
  123.5 2.7 fusion.224
  133.1 4.3 convolution_bitcast_fusion.6
  154.2 2.7 fusion.224
  163.8 4.3 convolution_bitcast_fusion.6
  185.0 2.7 fusion.224
  194.5 4.3 convolution_bitcast_fusion.6
  215.7 2.7 fusion.224
  225.3 4.3 convolution_bitcast_fusion.6
  246.4 2.7 fusion.224
  258.3 65.0 %all-reduce.2 = (f32[32]{0:T(128)S(1)}, f32[32]{0:T(128)S(1)}) all-reduce(f32[32]{0:T(128)S(1)} %dynamic-update-slice, f32[32]{0:T(128)S(1)} %dynamic-update-slice.1), channel_id=2, replica_groups=mesh['seq'=32,'head'=8] {'seq'}, use_global_device_ids=true, to_apply=%add | all-reduce | flops 64 | bytes 512
  323.3 35.0 %all-gather.4 = f32[32,1,256]{2,1,0:T(1,128)S(1)} all-gather(f32[1,1,256]{2,1,0:T(1,128)S(1)} %bitcast.818), channel_id=5, replica_groups=mesh['seq'=32,'head'=8] {'seq'}, dimensions={0}, use_global_device_ids=true | all-gather | bytes 33792 | tf_op jit(solution)/shard_map/all_gather | solution.py:17
  358.3 42.2 %all-gather.7.cloned.1.call-done = f32[32,256,512]{2,1,0:T(8,128)} async-done(((f32[1,256,512]{2,1,0:T(8,128)}), f32[32,256,512]{2,1,0:T(8,128)}) %all-gather.7.cloned.1.call-update) | async-done | bytes 16777232 | tf_op jit(solution)/shard_map/all_gather | solution.py:17
  400.5 130.6 %while.55 = (s32[]{:T(128)}, f32[1,256,512]{2,1,0:T(8,128)S(1)}, f32[1,256]{1,0:T(1,128)S(1)}, f32[1]{0:T(128)}, s32[]{:T(128)}, /*index=5*/f32[32,1]{0,1:T(1,12...) while((s32[]{:T(128)}, f32[1,256,512]{2,1,0:T(8,128)S(1)}, ...), condition=%wide.region_6.7_spmd.clone, body=%wide.region_5.6_spmd.clone.sunk | while | flops 656649 | bytes 1576196 | solution.py:26
  531.1 328.8 %while.53 = (s32[]{:T(128)}, f32[1,256,512]{2,1,0:T(8,128)S(1)}, f32[1,256]{1,0:T(1,128)S(1)}, f32[1]{0:T(128)}, f32[8,8,64,1,512]{4,2,1,3,0:T(8,128)}, /*index=...) while((s32[]{:T(128)}, f32[1,256,512]{2,1,0:T(8,128)S(1)}, ...), condition=%wide.region_13.14_spmd, body=%wide.region_7.13_spmd.sunk | while | flops 464969728 | bytes 78453536 | solution.py:180
  557.6 2.5 convert_element_type.261
  560.1 2.4 fusion.211
  563.1 3.2 fusion.212
  598.7 2.5 convert_element_type.261
  604.2 3.2 fusion.212
  611.0 2.4 fusion.217
  639.9 2.5 convert_element_type.261
  645.3 3.2 fusion.212
  681.0 2.5 convert_element_type.261
  683.4 2.4 fusion.211
  686.4 3.2 fusion.212
  722.1 2.5 convert_element_type.261
  727.5 3.2 fusion.212
  763.1 2.5 convert_element_type.261
  768.6 3.2 fusion.212
  804.3 2.5 convert_element_type.261
  806.7 2.4 fusion.211
  809.7 3.2 fusion.212
  845.4 2.5 convert_element_type.261
  850.8 3.2 fusion.212
  860.1 3.9 fusion.143
  864.0 54.3 %all_to_all.4 = bf16[8,512,512]{2,1,0:T(8,128)(2,1)} all-to-all(bf16[8,512,512]{2,1,0:T(8,128)(2,1)S(1)} %fusion.143), channel_id=1, replica_groups=mesh['seq'=32,'head'=8] {'head'}, dimensions={0} | all-to-all | bytes 8388608 | tf_op jit(solution)/shard_map/all_to_all | solution.py:186
  918.2 6.5 copy.26
  924.7 3.3 multiply_reduce_fusion
  928.1 2.4 fusion.142
  930.6 6.3 copy.27
  (494 shorter events, 245.2 us)
Async XLA Ops:
  6.5 394.0 %all-gather.7.cloned.1.call-start = ((), (), s32[]{:S(2)}) async-start(), calls=%async_computation.1 | async-start | bytes 17301504 | tf_op jit(solution)/shard_map/all_gather | solution.py:17
  9.4 246.8 %copy-start.5 = (u32[256]{0:T(256)S(1)}, u32[256]{0:T(256)}, u32[]{:S(2)}) copy-start(u32[256]{0:T(256)} %constant.99) | copy-start | bytes 3076
  255.3 0.8 copy-start.3
  534.1 18.5 %copy-start = (f32[1,8,256,512]{3,2,1,0:T(8,128)}, f32[1,8,256,512]{3,2,1,0:T(8,128)S(1)}, u32[]{:S(2)}) copy-start(f32[1,8,256,512]{3,2,1,0:T(8,128)S(1)} %convolution_bitcast_fusion.5) | copy-start | bytes 12582916 | tf_op jit(solution)/shard_map/while
  552.5 2.0 copy-start.1
  575.2 18.5 %copy-start = (f32[1,8,256,512]{3,2,1,0:T(8,128)}, f32[1,8,256,512]{3,2,1,0:T(8,128)S(1)}, u32[]{:S(2)}) copy-start(f32[1,8,256,512]{3,2,1,0:T(8,128)S(1)} %convolution_bitcast_fusion.5) | copy-start | bytes 12582916 | tf_op jit(solution)/shard_map/while
  593.6 2.0 copy-start.1
  616.3 18.5 %copy-start = (f32[1,8,256,512]{3,2,1,0:T(8,128)}, f32[1,8,256,512]{3,2,1,0:T(8,128)S(1)}, u32[]{:S(2)}) copy-start(f32[1,8,256,512]{3,2,1,0:T(8,128)S(1)} %convolution_bitcast_fusion.5) | copy-start | bytes 12582916 | tf_op jit(solution)/shard_map/while
  634.7 2.0 copy-start.1
  657.4 18.5 %copy-start = (f32[1,8,256,512]{3,2,1,0:T(8,128)}, f32[1,8,256,512]{3,2,1,0:T(8,128)S(1)}, u32[]{:S(2)}) copy-start(f32[1,8,256,512]{3,2,1,0:T(8,128)S(1)} %convolution_bitcast_fusion.5) | copy-start | bytes 12582916 | tf_op jit(solution)/shard_map/while
  675.8 2.0 copy-start.1
  698.5 18.5 %copy-start = (f32[1,8,256,512]{3,2,1,0:T(8,128)}, f32[1,8,256,512]{3,2,1,0:T(8,128)S(1)}, u32[]{:S(2)}) copy-start(f32[1,8,256,512]{3,2,1,0:T(8,128)S(1)} %convolution_bitcast_fusion.5) | copy-start | bytes 12582916 | tf_op jit(solution)/shard_map/while
  716.9 2.0 copy-start.1
  739.6 18.5 %copy-start = (f32[1,8,256,512]{3,2,1,0:T(8,128)}, f32[1,8,256,512]{3,2,1,0:T(8,128)S(1)}, u32[]{:S(2)}) copy-start(f32[1,8,256,512]{3,2,1,0:T(8,128)S(1)} %convolution_bitcast_fusion.5) | copy-start | bytes 12582916 | tf_op jit(solution)/shard_map/while
  758.0 2.0 copy-start.1
  780.7 18.5 %copy-start = (f32[1,8,256,512]{3,2,1,0:T(8,128)}, f32[1,8,256,512]{3,2,1,0:T(8,128)S(1)}, u32[]{:S(2)}) copy-start(f32[1,8,256,512]{3,2,1,0:T(8,128)S(1)} %convolution_bitcast_fusion.5) | copy-start | bytes 12582916 | tf_op jit(solution)/shard_map/while
  799.1 2.0 copy-start.1
  821.8 18.5 %copy-start = (f32[1,8,256,512]{3,2,1,0:T(8,128)}, f32[1,8,256,512]{3,2,1,0:T(8,128)S(1)}, u32[]{:S(2)}) copy-start(f32[1,8,256,512]{3,2,1,0:T(8,128)S(1)} %convolution_bitcast_fusion.5) | copy-start | bytes 12582916 | tf_op jit(solution)/shard_map/while
  840.2 2.0 copy-start.1
  918.2 9.8 %copy-start.4 = (f32[4096]{0:T(1024)S(1)}, f32[4096]{0:T(1024)}, u32[]{:S(2)}) copy-start(f32[4096]{0:T(1024)} %param.17) | copy-start | bytes 49156
  924.7 3.4 copy-start.2
Sparse Core Ops, SparseCore 0:
  256.3 144.2 all-gather.6
where the time goes:
time: 953 us; the launch traced here: 944 us
  loops' own time  356 us (37%)
  blocking collectives  154 us (16%)
  other arithmetic  153 us (16%)
  matrix products  144 us (15%)
  local copies, waits for them, and re-layouts  81.3 us (9%)
  waiting for transfers between devices  42.2 us (4%)
  between operations  13.5 us (1%)
    another operation x1, loops' own time, shards(): lax.scan(advance_states, empty_state, (key_blocks, value_blocks, input_bl...  165 us
    another operation x1, loops' own time, shards(): lax.scan(block_terms, (in_matrix, in_vector, in_level, zero_decay), feeds)  126 us
    unnamed x1, blocking collectives  65 us
    another operation x1, loops' own time, entering(): return lax.fori_loop(0, count - 1, hop, total)  64.8 us
    all_to_all x1, blocking collectives, shards(): lax.all_to_all(grouped, 'head', split_axis=0, concat_axis=2, tiled=True)  54.3 us
    dot_general x16, matrix products, block_states(): jnp.einsum('csjk,csjv->jckv', weighted, value_block, preferred_element_ty...  52 us
    select_n x62, other arithmetic, hop(): jnp.where(position < mine, new, old)  45.6 us
    all_gather x1, waiting for transfers between devices, entering(): pieces = jax.tree.map(lambda part: lax.all_gather(part, axis), value)  42.2 us
  transfers between devices with their start and end apart: 1, of which 1 were waited for; matrix products, arithmetic and copies ran while one was open for 0% of the time, Pallas kernels for 0%

commit v1 on v0

v1 whole, which is shorter than its diff:
```python
import functools

import jax
import jax.numpy as jnp
from jax import lax
from jax.experimental import pallas as pl
from jax.experimental.pallas import tpu as pltpu
from jax.sharding import PartitionSpec as P

EPSILON = 1e-06
FLOOR_LOG = -1e30
L = 256
EXT = 128
BF = jnp.bfloat16
F32 = jnp.float32
VMEM_LIMIT = 48 * 1024 * 1024


def dot(a, b):
    return jnp.dot(a, b, preferred_element_type=F32)


def pieces(x):
    hi = x.astype(BF).astype(F32)
    rest = x - hi
    mid = rest.astype(BF).astype(F32)
    return hi, mid, rest - mid


def ones_column(rows):
    return jnp.where(lax.broadcasted_iota(jnp.int32, (rows, EXT), 1) == 0, 1.0, 0.0).astype(BF)


def lay_columns(rows, columns):
    lane = lax.broadcasted_iota(jnp.int32, (rows, EXT), 1)
    out = jnp.zeros((rows, EXT), F32)
    for number, column in enumerate(columns):
        out = jnp.where(lane == number, column, out)
    return out


def gate_rows(forget_ref, input_ref, gates_ref, weight_ref, ends_ref):
    chunks = forget_ref.shape[0] * 128 // L

    def rows(ref):
        return jnp.concatenate(
            [ref[pl.ds(0, chunks, stride=2), :], ref[pl.ds(1, chunks, stride=2), :]], axis=1
        )

    forget = rows(forget_ref)
    lgate = jnp.minimum(forget, 0.0) - jnp.log1p(jnp.exp(-jnp.abs(forget)))
    lane = lax.broadcasted_iota(jnp.int32, (chunks, L), 1)
    within = lgate
    shift = 1
    while shift < L:
        within = within + jnp.where(lane >= shift, pltpu.roll(within, shift, 1), 0.0)
        shift *= 2
    lead = rows(input_ref) - within
    top = lead
    shift = 1
    while shift < L:
        top = jnp.maximum(top, jnp.where(lane >= shift, pltpu.roll(top, shift, 1), -jnp.inf))
        shift *= 2
    total = within[:, L - 1 :]
    chunk_top = total + top[:, L - 1 :]
    row = lax.broadcasted_iota(jnp.int32, (chunks, 1), 0)
    level = jnp.full((1, 1), FLOOR_LOG, F32)
    before = jnp.zeros((1, 1), F32)
    enter = jnp.zeros((chunks, 1), F32)
    leave = jnp.zeros((chunks, 1), F32)
    prefix = jnp.zeros((chunks, 1), F32)
    for c in range(chunks):
        enter = jnp.where(row == c, level, enter)
        prefix = jnp.where(row == c, before, prefix)
        level = jnp.maximum(level + total[c : c + 1], chunk_top[c : c + 1])
        before = before + total[c : c + 1]
        leave = jnp.where(row == c, level, leave)
    after = jnp.zeros((1, 1), F32)
    suffix = jnp.zeros((chunks, 1), F32)
    for c in reversed(range(chunks)):
        suffix = jnp.where(row == c, after, suffix)
        after = after + total[c : c + 1]
    carry = within + enter
    levels = jnp.maximum(within + top, carry)
    keylog = lead + total
    weight_ref[...] = jnp.exp(keylog + suffix - level)
    ends_ref[0:1, :] = jnp.broadcast_to(level, (1, 128))
    ends_ref[1:2, :] = jnp.broadcast_to(before, (1, 128))

    def put(number, value):
        for half in range(2):
            gates_ref[pl.ds(half * 8 + number, chunks, stride=16), :] = value[:, half * 128 : (half + 1) * 128]

    put(0, within - levels)
    put(1, jnp.exp(carry - levels))
    put(2, lead)
    put(3, jnp.exp(keylog - leave))
    put(4, within + prefix)
    put(5, levels)
    put(6, jnp.broadcast_to(jnp.exp(enter + total - leave), (chunks, L)))
    put(7, jnp.zeros((chunks, L), F32))


def local_state(forget_ref, input_ref, key_ref, value_ref, packet_ref, gates_ref, weight_ref, ends_ref, total_ref):
    step = pl.program_id(0)
    width = value_ref.shape[1]
    per = key_ref.shape[0] // L

    @pl.when(step == 0)
    def _():
        gate_rows(forget_ref, input_ref, gates_ref, weight_ref, ends_ref)
        total_ref[...] = jnp.zeros_like(total_ref)

    ones = ones_column(L)
    for part in range(per):
        span = slice(part * L, (part + 1) * L)
        weight = weight_ref[pl.ds(step * per + part, 1), :]
        weighted = (key_ref[span, :].T.astype(F32) * weight).astype(BF)
        total_ref[:, :width] += dot(weighted, value_ref[span, :])
        total_ref[:, width:] += dot(weighted, ones)

    @pl.when(step == pl.num_programs(0) - 1)
    def _():
        rows = total_ref.shape[0]
        packet_ref[:, :width] = total_ref[:, :width].astype(BF)
        vector = pieces(total_ref[:, width : width + 1])
        level = pieces(ends_ref[0:1, 0:1])
        decay = pieces(ends_ref[1:2, 0:1])
        packet_ref[:, width:] = lay_columns(rows, vector[:2] + level + decay).astype(BF)


def run_local_state(forget, inputs, keys, values):
    tokens, depth = keys.shape
    width = values.shape[1]
    block = 512
    chunks = tokens // L
    return pl.pallas_call(
        local_state,
        grid=(tokens // block,),
        in_specs=[
            pl.BlockSpec((tokens // 128, 128), lambda i: (0, 0)),
            pl.BlockSpec((tokens // 128, 128), lambda i: (0, 0)),
            pl.BlockSpec((block, depth), lambda i: (i, 0)),
            pl.BlockSpec((block, width), lambda i: (i, 0)),
        ],
        out_specs=[
            pl.BlockSpec((depth, width + EXT), lambda i: (0, 0)),
            pl.BlockSpec((chunks * 16, 128), lambda i: (0, 0)),
        ],
        out_shape=[
            jax.ShapeDtypeStruct((depth, width + EXT), BF),
            jax.ShapeDtypeStruct((chunks * 16, 128), F32),
        ],
        scratch_shapes=[
            pltpu.VMEM((chunks, L), F32),
            pltpu.VMEM((8, 128), F32),
            pltpu.VMEM((depth, width + EXT), F32),
        ],
        compiler_params=pltpu.CompilerParams(vmem_limit_bytes=VMEM_LIMIT),
        name="local_state",
    )(forget, inputs, keys, values)


def prefix_states(slices_ref, out_ref, *, count, each):
    wide = out_ref.shape[1]
    width = wide - EXT
    level = jnp.full((each, 1), FLOOR_LOG, F32)
    state = jnp.zeros((each, width), F32)
    vector = jnp.zeros((each, 1), F32)
    per = 16 // each
    for group in range(count // per):
        block = slices_ref[group * 16 : (group + 1) * 16, :].astype(F32)
        starts = []
        for number in range(per):
            mine = block[number * each : (number + 1) * each]

            def column(first, how_many):
                return sum(mine[:, width + first + n : width + first + n + 1] for n in range(how_many))

            hi, lo, _ = pieces(vector)
            starts.append(
                jnp.concatenate([state, lay_columns(each, (hi, lo) + pieces(level))], axis=1)
            )
            shifted = level + column(5, 3)
            later = column(2, 3)
            level = jnp.maximum(shifted, later)
            old, new = jnp.exp(shifted - level), jnp.exp(later - level)
            state = old * state + new * mine[:, :width]
            vector = old * vector + new * column(0, 2)
        out_ref[group * 16 : (group + 1) * 16, :] = jnp.concatenate(starts, axis=0).astype(BF)


def run_prefix(slices, count):
    rows, wide = slices.shape
    return pl.pallas_call(
        functools.partial(prefix_states, count=count, each=rows // count),
        out_shape=jax.ShapeDtypeStruct((rows, wide), BF),
        name="prefix_states",
    )(slices)


def local_outputs(gates_ref, query_ref, key_ref, value_ref, numer_ref, stats_ref, state_ref):
    width = value_ref.shape[1]

    @pl.when(pl.program_id(0) == 0)
    def _():
        state_ref[...] = jnp.zeros_like(state_ref)

    per = query_ref.shape[0] // L
    scale = 1.0 / query_ref.shape[1] ** 0.5
    causal = lax.broadcasted_iota(jnp.int32, (L, L), 0) >= lax.broadcasted_iota(jnp.int32, (L, L), 1)
    ones = ones_column(L)
    for part in range(per):
        span = slice(part * L, (part + 1) * L)
        gates = jnp.concatenate(
            [gates_ref[part * 16 + half * 8 : part * 16 + half * 8 + 8, :] for half in range(2)], axis=1
        )
        columns = gates.T
        query, key, value = query_ref[span, :], key_ref[span, :], value_ref[span, :]
        key_t = key.T
        scores = dot(query, key_t) * scale
        probs = jnp.where(causal, jnp.exp(columns[:, 0:1] + gates[2:3, :]) * scores, 0.0)
        far = columns[:, 1:2] * scale
        state = state_ref[...]
        high = state.astype(BF)
        low = (state - high.astype(F32)).astype(BF)
        carried = dot(query, high) + dot(query, low)
        numer_ref[span, :] = dot(probs.astype(BF), value) + far * carried[:, :width]
        denom = jnp.sum(probs, axis=1, keepdims=True) + far * carried[:, width : width + 1]
        stats_ref[span, :] = lay_columns(L, (denom, columns[:, 4:5], columns[:, 5:6]))
        weighted = (key_t.astype(F32) * gates[3:4, :]).astype(BF)
        old = gates[6:7, 0:1]
        state_ref[:, :width] = old * state[:, :width] + dot(weighted, value)
        state_ref[:, width:] = old * state[:, width:] + dot(weighted, ones)


def run_local_outputs(gates, queries, keys, values):
    tokens, depth = keys.shape
    width = values.shape[1]
    block = 512
    return pl.pallas_call(
        local_outputs,
        grid=(tokens // block,),
        in_specs=[
            pl.BlockSpec((block // L * 16, 128), lambda i: (i, 0)),
            pl.BlockSpec((block, depth), lambda i: (i, 0)),
            pl.BlockSpec((block, depth), lambda i: (i, 0)),
            pl.BlockSpec((block, width), lambda i: (i, 0)),
        ],
        out_specs=[
            pl.BlockSpec((block, width), lambda i: (i, 0)),
            pl.BlockSpec((block, EXT), lambda i: (i, 0)),
        ],
        out_shape=[
            jax.ShapeDtypeStruct((tokens, width), F32),
            jax.ShapeDtypeStruct((tokens, EXT), F32),
        ],
        scratch_shapes=[pltpu.VMEM((depth, width + EXT), F32)],
        compiler_params=pltpu.CompilerParams(vmem_limit_bytes=VMEM_LIMIT),
        name="local_outputs",
    )(gates, queries, keys, values)


def finish(place_ref, query_ref, numer_ref, stats_ref, packet_ref, hidden_ref):
    width = numer_ref.shape[1]
    scale = 1.0 / query_ref.shape[1] ** 0.5
    ends = packet_ref[0:16, width:].astype(F32)[0:1]
    entering = ends[:, 2:3] + ends[:, 3:4] + ends[:, 4:5]
    stats = stats_ref[...]
    carry = stats[:, 1:2] + entering
    level = jnp.maximum(stats[:, 2:3], carry)
    own = jnp.exp(stats[:, 2:3] - level)
    far = jnp.exp(carry - level) * scale
    reach = dot(query_ref[...], packet_ref[...])
    denom = own * stats[:, 0:1] + far * (reach[:, width : width + 1] + reach[:, width + 1 : width + 2])
    share = 1.0 / jnp.maximum(jnp.abs(denom), 1.0)
    hidden_ref[...] = ((own * numer_ref[...] + far * reach[:, :width]) * share).astype(BF)


def run_finish(place, queries, numer, stats, packet, owners):
    tokens, depth = queries.shape
    width = numer.shape[1]
    rows = tokens // owners

    def pick(i, place):
        return (place[0], 0)

    return pl.pallas_call(
        finish,
        grid_spec=pltpu.PrefetchScalarGridSpec(
            num_scalar_prefetch=1,
            grid=(1,),
            in_specs=[
                pl.BlockSpec((rows, depth), pick),
                pl.BlockSpec((rows, width), pick),
                pl.BlockSpec((rows, EXT), pick),
                pl.BlockSpec(packet.shape, lambda i, place: (0, 0)),
            ],
            out_specs=pl.BlockSpec((rows, width), lambda i, place: (0, 0)),
        ),
        out_shape=jax.ShapeDtypeStruct((rows, width), BF),
        compiler_params=pltpu.CompilerParams(vmem_limit_bytes=VMEM_LIMIT),
        cost_estimate=pl.CostEstimate(
            flops=2 * rows * depth * packet.shape[1],
            bytes_accessed=rows * (2 * depth + 6 * width + 512),
            transcendentals=0,
        ),
        name="finish",
    )(place, queries, numer, stats, packet)


def norm(place_ref, gain_ref, *refs):
    out_ref = refs[-1]
    parts = refs[:-1]
    count = len(parts)
    width = parts[0].shape[1]
    square = jnp.zeros((parts[0].shape[0], 128), F32)
    for part in parts:
        wide = part[...].astype(F32)
        wide = wide * wide
        for piece in range(width // 128):
            square = square + wide[:, piece * 128 : (piece + 1) * 128]
    mean = jnp.sum(square, axis=1, keepdims=True) / (count * width)
    factor = lax.rsqrt(mean + EPSILON)
    for hop, part in enumerate(parts):
        head = lax.rem(place_ref[0] - hop + count, count)
        columns = pl.ds(pl.multiple_of(head * width, width), width)
        out_ref[:, columns] = (part[...].astype(F32) * factor * gain_ref[:, columns]).astype(BF)


def run_norm(place, gain, parts):
    rows, width = parts[0].shape
    block = 128
    total = width * len(parts)
    return pl.pallas_call(
        norm,
        grid_spec=pltpu.PrefetchScalarGridSpec(
            num_scalar_prefetch=1,
            grid=(rows // block,),
            in_specs=[pl.BlockSpec((1, total), lambda i, place: (0, 0))]
            + [pl.BlockSpec((block, width), lambda i, place: (i, 0))] * len(parts),
            out_specs=pl.BlockSpec((block, total), lambda i, place: (i, 0)),
        ),
        out_shape=jax.ShapeDtypeStruct((rows, total), BF),
        compiler_params=pltpu.CompilerParams(vmem_limit_bytes=VMEM_LIMIT),
        name="norm",
    )(place, gain, *parts)


def swap_slices(packet, count):
    rows, wide = packet.shape
    cut = packet.reshape(count, rows // count, wide)
    return lax.all_to_all(cut, "seq", 0, 0, tiled=True).reshape(rows, wide)


def shards(queries, key_vectors, value_vectors, input_gate, forget_gate, norm_gain):
    tokens = queries.shape[0]
    queries, keys, values = (a.reshape(tokens, a.shape[2]) for a in (queries, key_vectors, value_vectors))
    forget = forget_gate.reshape(tokens // 128, 128)
    inputs = input_gate.reshape(tokens // 128, 128)
    count = lax.axis_size("seq")
    owners = lax.axis_size("head")
    mine = lax.axis_index("head").astype(jnp.int32).reshape(1)
    packet, gates = run_local_state(forget, inputs, keys, values)
    slices = swap_slices(packet, count)
    numer, stats = run_local_outputs(gates, queries, keys, values)
    entering = swap_slices(run_prefix(slices, count), count)
    parts = [None] * owners
    for hop in (4, 3, 5, 2, 6, 1, 7, 0):
        hidden = run_finish(lax.rem(mine + hop, owners), queries, numer, stats, entering, owners)
        if hop:
            hidden = lax.ppermute(hidden, "head", [(i, (i + hop) % owners) for i in range(owners)])
        parts[hop] = hidden
    return run_norm(mine, norm_gain.reshape(1, -1), parts)


def solution(mesh):
    in_specs = (
        P("seq", "head", None),
        P("seq", "head", None),
        P("seq", "head", None),
        P("head", "seq"),
        P("head", "seq"),
        P(),
    )
    out_specs = P(("seq", "head"), None)
    return jax.shard_map(shards, mesh=mesh, in_specs=in_specs, out_specs=out_specs, check_vma=False)
```

time: 953 us -> 121 us (0.13)
  loops' own time: 356 us -> 0 us
  other arithmetic: 153 us -> 0 us
  matrix products: 144 us -> 0 us
  blocking collectives: 154 us -> 22.1 us
  local copies, waits for them, and re-layouts: 81.3 us -> 6.09 us
  Pallas kernels: 0 us -> 43.9 us
  starting transfers between devices: 0.01 us -> 16.6 us
  between operations: 13.5 us -> 0.11 us
  waiting for transfers between devices: 42.2 us -> 31.3 us
    another operation x3 -> x0, loops' own time: 356 us -> none  [the longest x1 165 us: shards(): lax.scan(advance_states, empty_state, (key_blocks, value_blocks, input_bl...]
    dot_general x64 -> x0, matrix products: 144 us -> none  [the longest x16 52 us: block_states(): jnp.einsum('csjk,csjv->jckv', weighted, value_block, preferred_element_ty...]
    unnamed x1 -> x0, blocking collectives: 65 us -> none
    select_n x62 -> x0, other arithmetic: 45.6 us -> none  [hop(): jnp.where(position < mine, new, old)]
    pallas_call x0 -> x12, Pallas kernels: none -> 43.9 us  [the longest x8 17.1 us: run_finish(): pl.pallas_call(finish, grid_spec=pltpu.PrefetchScalarGridSpec(num_scalar_...]
    all_gather x1 -> x0, waiting for transfers between devices: 42.2 us -> none  [entering(): pieces = jax.tree.map(lambda part: lax.all_gather(part, axis), value)]
    all_gather x1 -> x0, blocking collectives: 35 us -> none  [entering(): pieces = jax.tree.map(lambda part: lax.all_gather(part, axis), value)]
    all_to_all x1, blocking collectives: 54.3 us -> 22.1 us  [swap_slices(): return lax.all_to_all(cut, 'seq', 0, 0, tiled=True).reshape(rows, wide)]
  transfers between devices with their start and end apart: 1 -> 8, of which waited for: 1 -> 6; matrix products, arithmetic and copies ran while one was open for 0% -> 0% of each run, Pallas kernels for 0% -> 23%
where the time goes in v1:
time: 121 us; the launch traced here: 120 us
  Pallas kernels  43.9 us (36%)
  waiting for transfers between devices  31.3 us (26%)
  blocking collectives  22.1 us (18%)
  starting transfers between devices  16.6 us (14%)
  local copies, waits for them, and re-layouts  6.09 us (5%)
    ppermute x7, waiting for transfers between devices, shards(): lax.ppermute(hidden, 'head', [(i, (i + hop) % owners) for i in range(owne...  31.3 us
    all_to_all x1, blocking collectives, swap_slices(): return lax.all_to_all(cut, 'seq', 0, 0, tiled=True).reshape(rows, wide)  22.1 us
    pallas_call x8, Pallas kernels, run_finish(): pl.pallas_call(finish, grid_spec=pltpu.PrefetchScalarGridSpec(num_scalar_...  17.1 us
    pallas_call x1, Pallas kernels, run_local_outputs(): pl.pallas_call(local_outputs, grid=(tokens // block,), in_specs=[pl.Block...  13.1 us
    ppermute x7, starting transfers between devices, shards(): lax.ppermute(hidden, 'head', [(i, (i + hop) % owners) for i in range(owne...  9.34 us
    pallas_call x1, Pallas kernels, run_local_state(): pl.pallas_call(local_state, grid=(tokens // block,), in_specs=[pl.BlockSp...  7.6 us
    all_to_all x1, starting transfers between devices, swap_slices(): return lax.all_to_all(cut, 'seq', 0, 0, tiled=True).reshape(rows, wide)  7.23 us
    unnamed x14, local copies, waits for them, and re-layouts  6.09 us
  transfers between devices with their start and end apart: 8, of which 6 were waited for; matrix products, arithmetic and copies ran while one was open for 0% of the time, Pallas kernels for 23%

profile of v1, /device:TPU:1, one launch (start us, length us, event | category | flops | bytes accessed | tf_op | source)
XLA Modules:
  0.0 120.1 jit_solution(10365668175829555191)
XLA Ops:
  0.0 0.0 copy-start
  0.0 0.0 copy-start.3
  0.0 1.7 %copy-done.3 = bf16[4096,1,256]{2,0,1:T(8,128)(2,1)S(1)} copy-done((bf16[4096,1,256]{2,0,1:T(8,128)(2,1)S(1)}, bf16[4096,1,256]{2,0,1:T(8,128)(2,1)}, u32[]{:S(2)}) %copy-start.3) | copy-done | bytes 2097176
  1.7 0.0 copy-start.4
  1.7 0.7 copy-done.4
  2.5 0.0 copy-start.5
  2.5 0.7 copy-done.5
  3.2 7.6 %local_state.1 = (bf16[256,640]{1,0:T(8,128)(2,1)S(1)}, f32[256,128]{1,0:T(8,128)S(1)}) custom-call(f32[32,128]{1,0:T(8,128)S(1)} %bitcast.31, f32[32,128]{1,0:T(8,128)S(1)} %bitcast.32, bf16[4096,256]{1,0:T(8,128)(2,1)S(1)} %bitcast.29, bf16[4096,512]{1,0:T(8,128)(2,1)} %bitcast.34), custom_call_target="tpu_custom_call" | custom-call | tf_op jit(solution)/shard_map/local_state/pallas_call | solution.py:137
  10.8 22.1 %all_to_all.10 = bf16[32,8,640]{2,1,0:T(8,128)(2,1)} all-to-all(bf16[32,8,640]{2,1,0:T(8,128)(2,1)S(1)} %bitcast.30), channel_id=1, replica_groups=mesh['seq'=32,'head'=8] {'seq'}, dimensions={0} | all-to-all | bytes 655360 | tf_op jit(solution)/shard_map/all_to_all | solution.py:353
  32.9 2.6 %prefix_states.1 = bf16[256,640]{1,0:T(8,128)(2,1)} custom-call(bf16[256,640]{1,0:T(8,128)(2,1)} %bitcast.37), custom_call_target="tpu_custom_call" | custom-call | tf_op jit(solution)/shard_map/prefix_states/pallas_call | solution.py:195
  35.5 7.2 %all-to-all-start.1 = ((bf16[32,8,640]{2,1,0:T(8,128)(2,1)}), bf16[32,8,640]{2,1,0:T(8,128)(2,1)S(1)}, u32[]{:S(2)}, u32[]{:S(2)}) async-start(bf16[32,8,640]{2,1,0:T(8,128)(2,1)} %bitcast.36), calls=%async_computation.1 | async-start | bytes 655360 | tf_op jit(solution)/shard_map/all_to_all | solution.py:353
  42.7 0.0 copy-done
  42.8 13.1 %local_outputs.1 = (f32[4096,512]{1,0:T(8,128)}, f32[4096,128]{1,0:T(8,128)S(1)}) custom-call(f32[256,128]{1,0:T(8,128)S(1)} %get-tuple-element.9.gates_ref, bf16[4096,256]{1,0:T(8,128)(2,1)S(1)} %bitcast.11, bf16[4096,256]{1,0:T(8,128)(2,1)} %bitcast.28, bf16[4096,512]{1,0:T(8,128)(2,1)} %bitcast.35), custom_call_target="tpu_custom_call" | custom-call | tf_op jit(solution)/shard_map/local_outputs/pallas_call | solution.py:241
  55.9 0.0 copy-start.1
  55.9 1.3 %copy-done.1 = f32[4096,128]{1,0:T(8,128)} copy-done((f32[4096,128]{1,0:T(8,128)}, f32[4096,128]{1,0:T(8,128)S(1)}, u32[]{:S(2)}) %copy-start.1) | copy-done | bytes 2097176
  57.2 0.0 all-to-all-done.1
  57.2 0.0 copy-start.2
  57.2 1.6 %copy-done.2 = f32[4096,128]{1,0:T(8,128)S(1)} copy-done((f32[4096,128]{1,0:T(8,128)S(1)}, f32[4096,128]{1,0:T(8,128)}, u32[]{:S(2)}) %copy-start.2) | copy-done | bytes 2097176
  58.8 2.1 %finish.9 = bf16[512,512]{1,0:T(8,128)(2,1)S(1)} custom-call(s32[1]{0:T(128)S(6)} %rem.115.place_ref, bf16[4096,256]{1,0:T(8,128)(2,1)S(1)} %bitcast.12, f32[4096,512]{1,0:T(8,128)} %get-tuple-element.10.numer_ref, f32[4096,128]{1,0:T(8,128)S(1)} %copy-done.2, bf16[256,640]{1,0:T(8,128)(2,1)S(1)} %bitcast.20), custom_call_target="tpu_custom_call" | custom-call | flops 167772160 | bytes 2097152 | tf_op jit(solution)/shard_map/finish/pallas_call | solution.py:288
  60.9 2.9 %collective-permute-start = (bf16[512,512]{1,0:T(8,128)(2,1)S(1)}, bf16[512,512]{1,0:T(8,128)(2,1)S(1)}, u32[]{:S(2)}, u32[]{:S(2)}) collective-permute-start(bf16[512,512]{1,0:T(8,128)(2,1)S(1)} %finish.9), channel_id=1, source_target_pairs={{0,1},{1,2},{2,3},{3,4},{4,5},{5,6},{6,7},{7,0},{8,9},{9,10},{10,1... | collective-permute-start | bytes 1572872 | tf_op jit(solution)/shard_map/ppermute | solution.py:372
  63.9 2.1 %finish.10 = bf16[512,512]{1,0:T(8,128)(2,1)S(1)} custom-call(s32[1]{0:T(128)S(6)} %rem.121.place_ref, bf16[4096,256]{1,0:T(8,128)(2,1)S(1)} %bitcast.13, f32[4096,512]{1,0:T(8,128)} %get-tuple-element.10.numer_ref, f32[4096,128]{1,0:T(8,128)S(1)} %copy-done.2, bf16[256,640]{1,0:T(8,128)(2,1)S(1)} %bitcast.21), custom_call_target="tpu_custom_call" | custom-call | flops 167772160 | bytes 2097152 | tf_op jit(solution)/shard_map/finish/pallas_call | solution.py:288
  66.0 1.3 %collective-permute-start.1 = (bf16[512,512]{1,0:T(8,128)(2,1)S(1)}, bf16[512,512]{1,0:T(8,128)(2,1)S(1)}, u32[]{:S(2)}, u32[]{:S(2)}) collective-permute-start(bf16[512,512]{1,0:T(8,128)(2,1)S(1)} %finish.10), channel_id=1, source_target_pairs={{0,2},{1,3},{2,4},{3,5},{4,6},{5,7},{6,0},{7,1},{8,10},{9,11},{10,... | collective-permute-start | bytes 1572872 | tf_op jit(solution)/shard_map/ppermute | solution.py:372
  67.3 2.1 %finish.11 = bf16[512,512]{1,0:T(8,128)(2,1)S(1)} custom-call(s32[1]{0:T(128)S(6)} %rem.127.place_ref, bf16[4096,256]{1,0:T(8,128)(2,1)S(1)} %bitcast.14, f32[4096,512]{1,0:T(8,128)} %get-tuple-element.10.numer_ref, f32[4096,128]{1,0:T(8,128)S(1)} %copy-done.2, bf16[256,640]{1,0:T(8,128)(2,1)S(1)} %bitcast.22), custom_call_target="tpu_custom_call" | custom-call | flops 167772160 | bytes 2097152 | tf_op jit(solution)/shard_map/finish/pallas_call | solution.py:288
  69.4 1.6 %collective-permute-start.2 = (bf16[512,512]{1,0:T(8,128)(2,1)S(1)}, bf16[512,512]{1,0:T(8,128)(2,1)S(1)}, u32[]{:S(2)}, u32[]{:S(2)}) collective-permute-start(bf16[512,512]{1,0:T(8,128)(2,1)S(1)} %finish.11), channel_id=1, source_target_pairs={{0,3},{1,4},{2,5},{3,6},{4,7},{5,0},{6,1},{7,2},{8,11},{9,12},{10,... | collective-permute-start | bytes 1572872 | tf_op jit(solution)/shard_map/ppermute | solution.py:372
  71.0 2.1 %finish.12 = bf16[512,512]{1,0:T(8,128)(2,1)S(1)} custom-call(s32[1]{0:T(128)S(6)} %rem.133.place_ref, bf16[4096,256]{1,0:T(8,128)(2,1)S(1)} %bitcast.15, f32[4096,512]{1,0:T(8,128)} %get-tuple-element.10.numer_ref, f32[4096,128]{1,0:T(8,128)S(1)} %copy-done.2, bf16[256,640]{1,0:T(8,128)(2,1)S(1)} %bitcast.23), custom_call_target="tpu_custom_call" | custom-call | flops 167772160 | bytes 2097152 | tf_op jit(solution)/shard_map/finish/pallas_call | solution.py:288
  73.2 0.6 collective-permute-start.3
  73.8 2.1 %finish.15 = bf16[512,512]{1,0:T(8,128)(2,1)S(1)} custom-call(s32[1]{0:T(128)S(6)} %rem.151.place_ref, bf16[4096,256]{1,0:T(8,128)(2,1)S(1)} %bitcast.16, f32[4096,512]{1,0:T(8,128)} %get-tuple-element.10.numer_ref, f32[4096,128]{1,0:T(8,128)S(1)} %copy-done.2, bf16[256,640]{1,0:T(8,128)(2,1)S(1)} %bitcast.24), custom_call_target="tpu_custom_call" | custom-call | flops 167772160 | bytes 2097152 | tf_op jit(solution)/shard_map/finish/pallas_call | solution.py:288
  75.9 2.1 %finish.14 = bf16[512,512]{1,0:T(8,128)(2,1)S(1)} custom-call(s32[1]{0:T(128)S(6)} %rem.145.place_ref, bf16[4096,256]{1,0:T(8,128)(2,1)S(1)} %bitcast.17, f32[4096,512]{1,0:T(8,128)} %get-tuple-element.10.numer_ref, f32[4096,128]{1,0:T(8,128)S(1)} %copy-done.2, bf16[256,640]{1,0:T(8,128)(2,1)S(1)} %bitcast.25), custom_call_target="tpu_custom_call" | custom-call | flops 167772160 | bytes 2097152 | tf_op jit(solution)/shard_map/finish/pallas_call | solution.py:288
  78.1 2.1 %finish.13 = bf16[512,512]{1,0:T(8,128)(2,1)S(1)} custom-call(s32[1]{0:T(128)S(6)} %rem.139.place_ref, bf16[4096,256]{1,0:T(8,128)(2,1)S(1)} %bitcast.18, f32[4096,512]{1,0:T(8,128)} %get-tuple-element.10.numer_ref, f32[4096,128]{1,0:T(8,128)S(1)} %copy-done.2, bf16[256,640]{1,0:T(8,128)(2,1)S(1)} %bitcast.26), custom_call_target="tpu_custom_call" | custom-call | flops 167772160 | bytes 2097152 | tf_op jit(solution)/shard_map/finish/pallas_call | solution.py:288
  80.2 2.3 %collective-permute-start.4 = (bf16[512,512]{1,0:T(8,128)(2,1)S(1)}, bf16[512,512]{1,0:T(8,128)(2,1)S(1)}, u32[]{:S(2)}, u32[]{:S(2)}) collective-permute-start(bf16[512,512]{1,0:T(8,128)(2,1)S(1)} %finish.13), channel_id=1, source_target_pairs={{0,5},{1,6},{2,7},{3,0},{4,1},{5,2},{6,3},{7,4},{8,13},{9,14},{10,... | collective-permute-start | bytes 1572872 | tf_op jit(solution)/shard_map/ppermute | solution.py:372
  82.5 0.0 collective-permute-done.refs_1_
  82.5 0.7 collective-permute-start.5
  83.1 2.7 %collective-permute-done.1.refs_2_ = bf16[512,512]{1,0:T(8,128)(2,1)S(1)} collective-permute-done((bf16[512,512]{1,0:T(8,128)(2,1)S(1)}, bf16[512,512]{1,0:T(8,128)(2,1)S(1)}, u32[]{:S(2)}, u32[]{:S(2)}) %collective-permute-start.1) | collective-permute-done | bytes 524320 | tf_op jit(solution)/shard_map/ppermute | solution.py:372
  85.9 0.0 collective-permute-start.6
  85.9 0.0 copy-start.6
  85.9 2.1 %finish.8.refs_0_ = bf16[512,512]{1,0:T(8,128)(2,1)S(1)} custom-call(s32[1]{0:T(128)S(6)} %rem.109.place_ref, bf16[4096,256]{1,0:T(8,128)(2,1)S(1)} %bitcast.19, f32[4096,512]{1,0:T(8,128)} %get-tuple-element.10.numer_ref, f32[4096,128]{1,0:T(8,128)S(1)} %copy-done.2, bf16[256,640]{1,0:T(8,128)(2,1)S(1)} %bitcast.27), custom_call_target="tpu_custom_call" | custom-call | flops 167772160 | bytes 2097152 | tf_op jit(solution)/shard_map/finish/pallas_call | solution.py:288
  88.0 7.2 %collective-permute-done.2.refs_3_ = bf16[512,512]{1,0:T(8,128)(2,1)S(1)} collective-permute-done((bf16[512,512]{1,0:T(8,128)(2,1)S(1)}, bf16[512,512]{1,0:T(8,128)(2,1)S(1)}, u32[]{:S(2)}, u32[]{:S(2)}) %collective-permute-start.2) | collective-permute-done | bytes 524320 | tf_op jit(solution)/shard_map/ppermute | solution.py:372
  95.2 14.1 %collective-permute-done.3.refs_4_ = bf16[512,512]{1,0:T(8,128)(2,1)S(1)} collective-permute-done((bf16[512,512]{1,0:T(8,128)(2,1)S(1)}, bf16[512,512]{1,0:T(8,128)(2,1)S(1)}, u32[]{:S(2)}, u32[]{:S(2)}) %collective-permute-start.3) | collective-permute-done | bytes 524320 | tf_op jit(solution)/shard_map/ppermute | solution.py:372
  109.3 2.9 %collective-permute-done.4.refs_5_ = bf16[512,512]{1,0:T(8,128)(2,1)S(1)} collective-permute-done((bf16[512,512]{1,0:T(8,128)(2,1)S(1)}, bf16[512,512]{1,0:T(8,128)(2,1)S(1)}, u32[]{:S(2)}, u32[]{:S(2)}) %collective-permute-start.4) | collective-permute-done | bytes 524320 | tf_op jit(solution)/shard_map/ppermute | solution.py:372
  112.2 3.5 %collective-permute-done.5.refs_6_ = bf16[512,512]{1,0:T(8,128)(2,1)S(1)} collective-permute-done((bf16[512,512]{1,0:T(8,128)(2,1)S(1)}, bf16[512,512]{1,0:T(8,128)(2,1)S(1)}, u32[]{:S(2)}, u32[]{:S(2)}) %collective-permute-start.5) | collective-permute-done | bytes 524320 | tf_op jit(solution)/shard_map/ppermute | solution.py:372
  115.7 0.9 collective-permute-done.6.refs_7_
  116.6 0.0 copy-done.6
  116.6 3.5 %norm.1 = bf16[512,4096]{1,0:T(8,128)(2,1)} custom-call(s32[1]{0:T(128)} %bitcast.place_ref, f32[1,4096]{1,0:T(1,128)S(1)} %bitcast.33, bf16[512,512]{1,0:T(8,128)(2,1)S(1)} %finish.8.refs_0_, bf16[512,512]{1,0:T(8,128)(2,1)S(1)} %collective-permute-done.refs_1_, bf16[512,512]{1,0:T(8,128)(2,1)S(1)} %collective-permute-done.1.refs_2_, ...), custom_call_target="tpu_custom_call" | custom-call | tf_op jit(solution)/shard_map/norm/pallas_call | solution.py:335
Async XLA Ops:
  0.0 42.8 %copy-start = (bf16[4096,1,256]{2,0,1:T(8,128)(2,1)S(1)}, bf16[4096,1,256]{2,0,1:T(8,128)(2,1)}, u32[]{:S(2)}) copy-start(bf16[4096,1,256]{2,0,1:T(8,128)(2,1)} %param.6) | copy-start | bytes 6291460
  0.0 1.7 %copy-start.3 = (bf16[4096,1,256]{2,0,1:T(8,128)(2,1)S(1)}, bf16[4096,1,256]{2,0,1:T(8,128)(2,1)}, u32[]{:S(2)}) copy-start(bf16[4096,1,256]{2,0,1:T(8,128)(2,1)} %param.7) | copy-start | bytes 6291460
  1.7 0.7 copy-start.4
  2.5 0.7 copy-start.5
  35.5 21.7 %all-to-all-start.1 = ((bf16[32,8,640]{2,1,0:T(8,128)(2,1)}), bf16[32,8,640]{2,1,0:T(8,128)(2,1)S(1)}, u32[]{:S(2)}, u32[]{:S(2)}) async-start(bf16[32,8,640]{2,1,0:T(8,128)(2,1)} %bitcast.36), calls=%async_computation.1 | async-start | bytes 655360 | tf_op jit(solution)/shard_map/all_to_all | solution.py:353
  55.9 1.3 %copy-start.1 = (f32[4096,128]{1,0:T(8,128)}, f32[4096,128]{1,0:T(8,128)S(1)}, u32[]{:S(2)}) copy-start(f32[4096,128]{1,0:T(8,128)S(1)} %get-tuple-element.11.stats_ref) | copy-start | bytes 6291460
  57.2 1.6 %copy-start.2 = (f32[4096,128]{1,0:T(8,128)S(1)}, f32[4096,128]{1,0:T(8,128)}, u32[]{:S(2)}) copy-start(f32[4096,128]{1,0:T(8,128)} %copy-done.1) | copy-start | bytes 6291460
  60.9 21.5 %collective-permute-start = (bf16[512,512]{1,0:T(8,128)(2,1)S(1)}, bf16[512,512]{1,0:T(8,128)(2,1)S(1)}, u32[]{:S(2)}, u32[]{:S(2)}) collective-permute-start(bf16[512,512]{1,0:T(8,128)(2,1)S(1)} %finish.9), channel_id=1, source_target_pairs={{0,1},{1,2},{2,3},{3,4},{4,5},{5,6},{6,7},{7,0},{8,9},{9,10},{10,1... | collective-permute-start | bytes 1572872 | tf_op jit(solution)/shard_map/ppermute | solution.py:372
  66.0 19.9 %collective-permute-start.1 = (bf16[512,512]{1,0:T(8,128)(2,1)S(1)}, bf16[512,512]{1,0:T(8,128)(2,1)S(1)}, u32[]{:S(2)}, u32[]{:S(2)}) collective-permute-start(bf16[512,512]{1,0:T(8,128)(2,1)S(1)} %finish.10), channel_id=1, source_target_pairs={{0,2},{1,3},{2,4},{3,5},{4,6},{5,7},{6,0},{7,1},{8,10},{9,11},{10,... | collective-permute-start | bytes 1572872 | tf_op jit(solution)/shard_map/ppermute | solution.py:372
  69.4 25.8 %collective-permute-start.2 = (bf16[512,512]{1,0:T(8,128)(2,1)S(1)}, bf16[512,512]{1,0:T(8,128)(2,1)S(1)}, u32[]{:S(2)}, u32[]{:S(2)}) collective-permute-start(bf16[512,512]{1,0:T(8,128)(2,1)S(1)} %finish.11), channel_id=1, source_target_pairs={{0,3},{1,4},{2,5},{3,6},{4,7},{5,0},{6,1},{7,2},{8,11},{9,12},{10,... | collective-permute-start | bytes 1572872 | tf_op jit(solution)/shard_map/ppermute | solution.py:372
  73.2 36.1 %collective-permute-start.3 = (bf16[512,512]{1,0:T(8,128)(2,1)S(1)}, bf16[512,512]{1,0:T(8,128)(2,1)S(1)}, u32[]{:S(2)}, u32[]{:S(2)}) collective-permute-start(bf16[512,512]{1,0:T(8,128)(2,1)S(1)} %finish.12), channel_id=1, source_target_pairs={{0,4},{1,5},{2,6},{3,7},{4,0},{5,1},{6,2},{7,3},{8,12},{9,13},{10,... | collective-permute-start | bytes 1572872 | tf_op jit(solution)/shard_map/ppermute | solution.py:372
  80.2 32.0 %collective-permute-start.4 = (bf16[512,512]{1,0:T(8,128)(2,1)S(1)}, bf16[512,512]{1,0:T(8,128)(2,1)S(1)}, u32[]{:S(2)}, u32[]{:S(2)}) collective-permute-start(bf16[512,512]{1,0:T(8,128)(2,1)S(1)} %finish.13), channel_id=1, source_target_pairs={{0,5},{1,6},{2,7},{3,0},{4,1},{5,2},{6,3},{7,4},{8,13},{9,14},{10,... | collective-permute-start | bytes 1572872 | tf_op jit(solution)/shard_map/ppermute | solution.py:372
  82.5 33.2 %collective-permute-start.5 = (bf16[512,512]{1,0:T(8,128)(2,1)S(1)}, bf16[512,512]{1,0:T(8,128)(2,1)S(1)}, u32[]{:S(2)}, u32[]{:S(2)}) collective-permute-start(bf16[512,512]{1,0:T(8,128)(2,1)S(1)} %finish.14), channel_id=1, source_target_pairs={{0,6},{1,7},{2,0},{3,1},{4,2},{5,3},{6,4},{7,5},{8,14},{9,15},{10,... | collective-permute-start | bytes 1572872 | tf_op jit(solution)/shard_map/ppermute | solution.py:372
  85.9 30.7 %collective-permute-start.6 = (bf16[512,512]{1,0:T(8,128)(2,1)S(1)}, bf16[512,512]{1,0:T(8,128)(2,1)S(1)}, u32[]{:S(2)}, u32[]{:S(2)}) collective-permute-start(bf16[512,512]{1,0:T(8,128)(2,1)S(1)} %finish.15), channel_id=1, source_target_pairs={{0,7},{1,0},{2,1},{3,2},{4,3},{5,4},{6,5},{7,6},{8,15},{9,8},{10,9... | collective-permute-start | bytes 1572872 | tf_op jit(solution)/shard_map/ppermute | solution.py:372
  85.9 30.7 %copy-start.6 = (f32[4096]{0:T(1024)S(1)}, f32[4096]{0:T(1024)}, u32[]{:S(2)}) copy-start(f32[4096]{0:T(1024)} %param.11) | copy-start | bytes 49156

commit v2 on v1

--- a/solution.py
+++ b/solution.py
@@ -11,9 +11,14 @@
 FLOOR_LOG = -1e30
 L = 256
 EXT = 128
+BLOCKS = 4
 BF = jnp.bfloat16
 F32 = jnp.float32
-VMEM_LIMIT = 48 * 1024 * 1024
+VMEM_LIMIT = 60 * 1024 * 1024
+OUTPUTS_LIMIT = 60 * 1024 * 1024
+SMALL_LIMIT = 20 * 1024 * 1024
+FINISH_LIMIT = 24 * 1024 * 1024
+HOPS = ((4, 3), (5, 2, 6, 1, 7, 0))
 
 
 def dot(a, b):
@@ -101,60 +106,72 @@
     put(7, jnp.zeros((chunks, L), F32))
 
 
-def local_state(forget_ref, input_ref, key_ref, value_ref, packet_ref, gates_ref, weight_ref, ends_ref, total_ref):
-    step = pl.program_id(0)
+def fetch(pairs, sems):
+    waits = []
+    for row, blocks in enumerate(pairs):
+        started = []
+        for column, (source, target) in enumerate(blocks):
+            copy = pltpu.make_async_copy(source, target, sems.at[row, column])
+            copy.start()
+            started.append(copy)
+        waits.append(started)
+    return waits
+
+
+def local_state(
+    forget_ref, input_ref, key_hbm, value_hbm, packet_ref, gates_ref, key_ref, value_ref, weight_ref, ends_ref, sems
+):
+    tokens, rows = key_ref.shape
     width = value_ref.shape[1]
-    per = key_ref.shape[0] // L
-
-    @pl.when(step == 0)
-    def _():
-        gate_rows(forget_ref, input_ref, gates_ref, weight_ref, ends_ref)
-        total_ref[...] = jnp.zeros_like(total_ref)
-
-    ones = ones_column(L)
-    for part in range(per):
-        span = slice(part * L, (part + 1) * L)
-        weight = weight_ref[pl.ds(step * per + part, 1), :]
+    block = tokens // sems.shape[0]
+    spans = [pl.ds(number * block, block) for number in range(sems.shape[0])]
+    waits = fetch(
+        [
+            [(key_hbm.at[span, :], key_ref.at[span, :]), (value_hbm.at[span, :], value_ref.at[span, :])]
+            for span in spans
+        ],
+        sems,
+    )
+    gate_rows(forget_ref, input_ref, gates_ref, weight_ref, ends_ref)
+    ones = ones_column(block)
+    per = block // L
+    matrix = vector = None
+    for number, span in enumerate(spans):
+        for copy in waits[number]:
+            copy.wait()
+        weight = jnp.concatenate(
+            [weight_ref[number * per + part : number * per + part + 1, :] for part in range(per)], axis=1
+        )
         weighted = (key_ref[span, :].T.astype(F32) * weight).astype(BF)
-        total_ref[:, :width] += dot(weighted, value_ref[span, :])
-        total_ref[:, width:] += dot(weighted, ones)
-
-    @pl.when(step == pl.num_programs(0) - 1)
-    def _():
-        rows = total_ref.shape[0]
-        packet_ref[:, :width] = total_ref[:, :width].astype(BF)
-        vector = pieces(total_ref[:, width : width + 1])
-        level = pieces(ends_ref[0:1, 0:1])
-        decay = pieces(ends_ref[1:2, 0:1])
-        packet_ref[:, width:] = lay_columns(rows, vector[:2] + level + decay).astype(BF)
+        add_matrix, add_vector = dot(weighted, value_ref[span, :]), dot(weighted, ones)
+        matrix = add_matrix if matrix is None else matrix + add_matrix
+        vector = add_vector if vector is None else vector + add_vector
+    packet_ref[:, :width] = matrix.astype(BF)
+    level = pieces(ends_ref[0:1, 0:1])
+    decay = pieces(ends_ref[1:2, 0:1])
+    packet_ref[:, width:] = lay_columns(rows, pieces(vector[:, 0:1])[:2] + level + decay).astype(BF)
 
 
 def run_local_state(forget, inputs, keys, values):
     tokens, depth = keys.shape
     width = values.shape[1]
-    block = 512
     chunks = tokens // L
+    vmem = pl.BlockSpec(memory_space=pltpu.VMEM)
+    hbm = pl.BlockSpec(memory_space=pl.ANY)
     return pl.pallas_call(
         local_state,
-        grid=(tokens // block,),
-        in_specs=[
-            pl.BlockSpec((tokens // 128, 128), lambda i: (0, 0)),
-            pl.BlockSpec((tokens // 128, 128), lambda i: (0, 0)),
-            pl.BlockSpec((block, depth), lambda i: (i, 0)),
-            pl.BlockSpec((block, width), lambda i: (i, 0)),
-        ],
-        out_specs=[
-            pl.BlockSpec((depth, width + EXT), lambda i: (0, 0)),
-            pl.BlockSpec((chunks * 16, 128), lambda i: (0, 0)),
-        ],
+        in_specs=[vmem, vmem, hbm, hbm],
+        out_specs=[vmem, vmem],
         out_shape=[
             jax.ShapeDtypeStruct((depth, width + EXT), BF),
             jax.ShapeDtypeStruct((chunks * 16, 128), F32),
         ],
         scratch_shapes=[
+            pltpu.VMEM((tokens, depth), BF),
+            pltpu.VMEM((tokens, width), BF),
             pltpu.VMEM((chunks, L), F32),
             pltpu.VMEM((8, 128), F32),
-            pltpu.VMEM((depth, width + EXT), F32),
+            pltpu.SemaphoreType.DMA((BLOCKS, 2)),
         ],
         compiler_params=pltpu.CompilerParams(vmem_limit_bytes=VMEM_LIMIT),
         name="local_state",
@@ -195,16 +212,19 @@
     return pl.pallas_call(
         functools.partial(prefix_states, count=count, each=rows // count),
         out_shape=jax.ShapeDtypeStruct((rows, wide), BF),
+        compiler_params=pltpu.CompilerParams(vmem_limit_bytes=SMALL_LIMIT),
         name="prefix_states",
     )(slices)
 
 
-def local_outputs(gates_ref, query_ref, key_ref, value_ref, numer_ref, stats_ref, state_ref):
+def local_outputs(gates_ref, query_ref, key_ref, value_ref, *refs):
+    start_ref = refs[-4] if len(refs) == 6 else None
+    numer_ref, stats_ref, state_ref = refs[-3:]
     width = value_ref.shape[1]
 
     @pl.when(pl.program_id(0) == 0)
     def _():
-        state_ref[...] = jnp.zeros_like(state_ref)
+        state_ref[...] = jnp.zeros_like(state_ref) if start_ref is None else start_ref[...]
 
     per = query_ref.shape[0] // L
     scale = 1.0 / query_ref.shape[1] ** 0.5
@@ -225,88 +245,137 @@
         high = state.astype(BF)
         low = (state - high.astype(F32)).astype(BF)
         carried = dot(query, high) + dot(query, low)
-        numer_ref[span, :] = dot(probs.astype(BF), value) + far * carried[:, :width]
+        numer_ref[span, :] = (dot(probs.astype(BF), value) + far * carried[:, :width]).astype(BF)
         denom = jnp.sum(probs, axis=1, keepdims=True) + far * carried[:, width : width + 1]
-        stats_ref[span, :] = lay_columns(L, (denom, columns[:, 4:5], columns[:, 5:6]))
+        flat = lay_columns(L, (denom,)).T[:8]
+        for half in range(2):
+            first = part * 16 + half * 8
+            stats_ref[first : first + 8, :] = flat[:, half * 128 : (half + 1) * 128]
         weighted = (key_t.astype(F32) * gates[3:4, :]).astype(BF)
         old = gates[6:7, 0:1]
         state_ref[:, :width] = old * state[:, :width] + dot(weighted, value)
         state_ref[:, width:] = old * state[:, width:] + dot(weighted, ones)
 
 
-def run_local_outputs(gates, queries, keys, values):
+def run_local_outputs(gates, queries, keys, values, half, before=None):
     tokens, depth = keys.shape
     width = values.shape[1]
-    block = 512
+    block = 1024
+    steps = tokens // block // 2
+    first = half * steps
+
+    def at(i):
+        return (first + i, 0)
+
+    whole = pl.BlockSpec((depth, width + EXT), lambda i: (0, 0))
     return pl.pallas_call(
         local_outputs,
-        grid=(tokens // block,),
+        grid=(steps,),
         in_specs=[
-            pl.BlockSpec((block // L * 16, 128), lambda i: (i, 0)),
-            pl.BlockSpec((block, depth), lambda i: (i, 0)),
-            pl.BlockSpec((block, depth), lambda i: (i, 0)),
-            pl.BlockSpec((block, width), lambda i: (i, 0)),
-        ],
+            pl.BlockSpec((block // L * 16, 128), at),
+            pl.BlockSpec((block, depth), at),
+            pl.BlockSpec((block, depth), at),
+            pl.BlockSpec((block, width), at),
+        ]
+        + ([pl.BlockSpec(memory_space=pl.ANY)] * 2 + [whole] if half else []),
         out_specs=[
-            pl.BlockSpec((block, width), lambda i: (i, 0)),
-            pl.BlockSpec((block, EXT), lambda i: (i, 0)),
+            pl.BlockSpec((block, width), at),
+            pl.BlockSpec((block // L * 16, 128), at),
+            whole,
         ],
         out_shape=[
-            jax.ShapeDtypeStruct((tokens, width), F32),
-            jax.ShapeDtypeStruct((tokens, EXT), F32),
-        ],
-        scratch_shapes=[pltpu.VMEM((depth, width + EXT), F32)],
-        compiler_params=pltpu.CompilerParams(vmem_limit_bytes=VMEM_LIMIT),
+            jax.ShapeDtypeStruct((tokens, width), BF),
+            jax.ShapeDtypeStruct((tokens // L * 16, 128), F32),
+            jax.ShapeDtypeStruct((depth, width + EXT), F32),
+        ],
+        input_output_aliases={4: 0, 5: 1} if half else {},
+        compiler_params=pltpu.CompilerParams(vmem_limit_bytes=OUTPUTS_LIMIT),
         name="local_outputs",
-    )(gates, queries, keys, values)
-
-
-def finish(place_ref, query_ref, numer_ref, stats_ref, packet_ref, hidden_ref):
-    width = numer_ref.shape[1]
-    scale = 1.0 / query_ref.shape[1] ** 0.5
+    )(gates, queries, keys, values, *(before or ()))
+
+
+def finish(
+    place_ref, query_hbm, numer_hbm, gates_ref, stats_ref, packet_ref, *refs, hops, owners
+):
+    outs = refs[: len(hops)]
+    query_ref, numer_ref, hidden_ref, in_sems, out_sems = refs[len(hops) :]
+    rows = query_ref.shape[1]
+    width = numer_ref.shape[2]
+    scale = 1.0 / query_ref.shape[2] ** 0.5
+    targets = [lax.rem(place_ref[0] + hop, owners) for hop in hops]
+    blocks = []
+    for number, target in enumerate(targets):
+        span = pl.ds(pl.multiple_of(target * rows, rows), rows)
+        blocks.append(
+            [(query_hbm.at[span, :], query_ref.at[number]), (numer_hbm.at[span, :], numer_ref.at[number])]
+        )
+    waits = fetch(blocks, in_sems)
     ends = packet_ref[0:16, width:].astype(F32)[0:1]
     entering = ends[:, 2:3] + ends[:, 3:4] + ends[:, 4:5]
-    stats = stats_ref[...]
-    carry = stats[:, 1:2] + entering
-    level = jnp.maximum(stats[:, 2:3], carry)
-    own = jnp.exp(stats[:, 2:3] - level)
-    far = jnp.exp(carry - level) * scale
-    reach = dot(query_ref[...], packet_ref[...])
-    denom = own * stats[:, 0:1] + far * (reach[:, width : width + 1] + reach[:, width + 1 : width + 2])
-    share = 1.0 / jnp.maximum(jnp.abs(denom), 1.0)
-    hidden_ref[...] = ((own * numer_ref[...] + far * reach[:, :width]) * share).astype(BF)
-
-
-def run_finish(place, queries, numer, stats, packet, owners):
+    copies = []
+    for number, target in enumerate(targets):
+        for copy in waits[number]:
+            copy.wait()
+        tall = rows // L * 16
+        tile = pl.ds(pl.multiple_of(target * tall, tall), tall)
+        gates, stats = gates_ref[tile, :], stats_ref[tile, :]
+        row = lax.broadcasted_iota(jnp.int32, (8, L), 0)
+        for part in range(rows // L):
+            span = slice(part * L, (part + 1) * L)
+
+            def rows_of(array):
+                first = part * 16
+                return jnp.concatenate([array[first : first + 8], array[first + 8 : first + 16]], axis=1)
+
+            marks, sums = rows_of(gates), rows_of(stats)
+            local = marks[5:6]
+            carry = marks[4:5] + entering
+            level = jnp.maximum(local, carry)
+            own = jnp.exp(local - level)
+            far = jnp.exp(carry - level) * scale
+            columns = jnp.where(row == 0, own, jnp.where(row == 1, far, own * sums[0:1])).T
+            own, far = columns[:, 0:1], columns[:, 1:2]
+            reach = dot(query_ref[number, span, :], packet_ref[...])
+            vector = reach[:, width : width + 1] + reach[:, width + 1 : width + 2]
+            share = 1.0 / jnp.maximum(jnp.abs(columns[:, 2:3] + far * vector), 1.0)
+            hidden_ref[number, span, :] = (
+                (own * share) * numer_ref[number, span, :].astype(F32) + (far * share) * reach[:, :width]
+            ).astype(BF)
+        copy = pltpu.make_async_copy(hidden_ref.at[number], outs[number], out_sems.at[number])
+        copy.start()
+        copies.append(copy)
+    for copy in copies:
+        copy.wait()
+
+
+def run_finish(place, queries, numer, gates, stats, packet, owners, hops):
     tokens, depth = queries.shape
     width = numer.shape[1]
     rows = tokens // owners
-
-    def pick(i, place):
-        return (place[0], 0)
-
+    count = len(hops)
+    vmem = pl.BlockSpec(memory_space=pltpu.VMEM)
+    hbm = pl.BlockSpec(memory_space=pltpu.HBM)
+    anywhere = pl.BlockSpec(memory_space=pl.ANY)
     return pl.pallas_call(
-        finish,
-        grid_spec=pltpu.PrefetchScalarGridSpec(
-            num_scalar_prefetch=1,
-            grid=(1,),
-            in_specs=[
-                pl.BlockSpec((rows, depth), pick),
-                pl.BlockSpec((rows, width), pick),
-                pl.BlockSpec((rows, EXT), pick),
-                pl.BlockSpec(packet.shape, lambda i, place: (0, 0)),
-            ],
-            out_specs=pl.BlockSpec((rows, width), lambda i, place: (0, 0)),
-        ),
-        out_shape=jax.ShapeDtypeStruct((rows, width), BF),
-        compiler_params=pltpu.CompilerParams(vmem_limit_bytes=VMEM_LIMIT),
+        functools.partial(finish, hops=hops, owners=owners),
+        in_specs=[pl.BlockSpec(memory_space=pltpu.SMEM), hbm, hbm, vmem, vmem, vmem],
+        out_specs=[anywhere] * count,
+        out_shape=[jax.ShapeDtypeStruct((rows, width), BF)] * count,
+        scratch_shapes=[
+            pltpu.VMEM((count, rows, depth), BF),
+            pltpu.VMEM((count, rows, width), BF),
+            pltpu.VMEM((count, rows, width), BF),
+            pltpu.SemaphoreType.DMA((count, 2)),
+            pltpu.SemaphoreType.DMA((count,)),
+        ],
+        compiler_params=pltpu.CompilerParams(vmem_limit_bytes=FINISH_LIMIT),
         cost_estimate=pl.CostEstimate(
-            flops=2 * rows * depth * packet.shape[1],
-            bytes_accessed=rows * (2 * depth + 6 * width + 512),
+            flops=2 * count * rows * depth * packet.shape[1],
+            bytes_accessed=count * rows * (2 * depth + 4 * width),
             transcendentals=0,
         ),
         name="finish",
-    )(place, queries, numer, stats, packet)
+    )(place, queries, numer, gates, stats, packet)
 
 
 def norm(place_ref, gain_ref, *refs):
@@ -342,7 +411,7 @@
             out_specs=pl.BlockSpec((block, total), lambda i, place: (i, 0)),
         ),
         out_shape=jax.ShapeDtypeStruct((rows, total), BF),
-        compiler_params=pltpu.CompilerParams(vmem_limit_bytes=VMEM_LIMIT),
+        compiler_params=pltpu.CompilerParams(vmem_limit_bytes=SMALL_LIMIT),
         name="norm",
     )(place, gain, *parts)
 
@@ -363,14 +432,20 @@
     mine = lax.axis_index("head").astype(jnp.int32).reshape(1)
     packet, gates = run_local_state(forget, inputs, keys, values)
     slices = swap_slices(packet, count)
-    numer, stats = run_local_outputs(gates, queries, keys, values)
-    entering = swap_slices(run_prefix(slices, count), count)
+    before = run_local_outputs(gates, queries, keys, values, 0)
+    slices, before = lax.optimization_barrier((slices, before))
+    starts = run_prefix(slices, count)
+    starts, before = lax.optimization_barrier((starts, before))
+    entering = swap_slices(starts, count)
+    numer, stats, _ = run_local_outputs(gates, queries, keys, values, 1, before)
     parts = [None] * owners
-    for hop in (4, 3, 5, 2, 6, 1, 7, 0):
-        hidden = run_finish(lax.rem(mine + hop, owners), queries, numer, stats, entering, owners)
-        if hop:
-            hidden = lax.ppermute(hidden, "head", [(i, (i + hop) % owners) for i in range(owners)])
-        parts[hop] = hidden
+    place = mine
+    for hops in HOPS:
+        group = run_finish(place, queries, numer, gates, stats, entering, owners, hops)
+        for hop, hidden in zip(hops, group):
+            if hop:
+                hidden = lax.ppermute(hidden, "head", [(i, (i + hop) % owners) for i in range(owners)])
+            parts[hop] = hidden
     return run_norm(mine, norm_gain.reshape(1, -1), parts)
 
 

time: 121 us -> 110 us (0.909)
  blocking collectives: 22.1 us -> 0 us
  starting transfers between devices: 16.6 us -> 30.3 us
  waiting for transfers between devices: 31.3 us -> 39.1 us
  Pallas kernels: 43.9 us -> 36.5 us
  local copies, waits for them, and re-layouts: 6.09 us -> 3.11 us
    all_to_all x1 -> x0, blocking collectives: 22.1 us -> none  [swap_slices(): return lax.all_to_all(cut, 'seq', 0, 0, tiled=True).reshape(rows, wide)]
    all_to_all x1 -> x2, starting transfers between devices: 7.23 us -> 19.3 us  [swap_slices(): return lax.all_to_all(cut, 'seq', 0, 0, tiled=True).reshape(rows, wide)]
    pallas_call x10 -> x5, Pallas kernels: 37.8 us -> 31.3 us  [the longest x2 16.3 us: run_local_outputs(): pl.pallas_call(local_outputs, grid=(steps,), in_specs=[pl.BlockSpec((bloc...]
    ppermute x7, waiting for transfers between devices: 31.3 us -> 35.4 us  [shards(): lax.ppermute(hidden, 'head', [(i, (i + hop) % owners) for i in range(owne...]
    all_to_all x1 -> x2, waiting for transfers between devices: 0.01 us -> 3.71 us  [swap_slices(): return lax.all_to_all(cut, 'seq', 0, 0, tiled=True).reshape(rows, wide)]
    unnamed x14 -> x10, local copies, waits for them, and re-layouts: 6.09 us -> 3.11 us
    ppermute x7, starting transfers between devices: 9.34 us -> 11.1 us  [shards(): lax.ppermute(hidden, 'head', [(i, (i + hop) % owners) for i in range(owne...]
  transfers between devices with their start and end apart: 8 -> 9, of which waited for: 6 -> 7; matrix products, arithmetic and copies ran while one was open for 0% -> 0% of each run, Pallas kernels for 23% -> 21%
where the time goes in v2:
time: 110 us; the launch traced here: 109 us
  waiting for transfers between devices  39.1 us (36%)
  Pallas kernels  36.5 us (33%)
  starting transfers between devices  30.3 us (28%)
  local copies, waits for them, and re-layouts  3.11 us (3%)
    ppermute x7, waiting for transfers between devices, shards(): lax.ppermute(hidden, 'head', [(i, (i + hop) % owners) for i in range(owne...  35.4 us
    all_to_all x2, starting transfers between devices, swap_slices(): return lax.all_to_all(cut, 'seq', 0, 0, tiled=True).reshape(rows, wide)  19.3 us
    pallas_call x2, Pallas kernels, run_local_outputs(): pl.pallas_call(local_outputs, grid=(steps,), in_specs=[pl.BlockSpec((bloc...  16.3 us
    ppermute x7, starting transfers between devices, shards(): lax.ppermute(hidden, 'head', [(i, (i + hop) % owners) for i in range(owne...  11.1 us
    pallas_call x2, Pallas kernels, run_finish(): pl.pallas_call(functools.partial(finish, hops=hops, owners=owners), in_sp...  9.24 us
    pallas_call x1, Pallas kernels, run_local_state(): pl.pallas_call(local_state, in_specs=[vmem, vmem, hbm, hbm], out_specs=[v...  5.76 us
    all_to_all x2, waiting for transfers between devices, swap_slices(): return lax.all_to_all(cut, 'seq', 0, 0, tiled=True).reshape(rows, wide)  3.71 us
    pallas_call x1, Pallas kernels, run_norm(): pl.pallas_call(norm, grid_spec=pltpu.PrefetchScalarGridSpec(num_scalar_pr...  3.53 us
  transfers between devices with their start and end apart: 9, of which 7 were waited for; matrix products, arithmetic and copies ran while one was open for 0% of the time, Pallas kernels for 21%

profile of v2, /device:TPU:1, one launch (start us, length us, event | category | flops | bytes accessed | tf_op | source)
XLA Modules:
  0.0 109.1 jit_solution(10515473755649437436)
XLA Ops:
  0.0 5.8 %local_state.1 = (bf16[256,640]{1,0:T(8,128)(2,1)}, f32[256,128]{1,0:T(8,128)}) custom-call(f32[32,128]{1,0:T(8,128)} %bitcast.26, f32[32,128]{1,0:T(8,128)} %bitcast.27, bf16[4096,256]{1,0:T(8,128)(2,1)} %bitcast.22, bf16[4096,512]{1,0:T(8,128)(2,1)} %bitcast.19), custom_call_target="tpu_custom_call" | custom-call | tf_op jit(solution)/shard_map/local_state/pallas_call | solution.py:161
  5.8 12.0 %all-to-all-start = ((bf16[32,8,640]{2,1,0:T(8,128)(2,1)}), bf16[32,8,640]{2,1,0:T(8,128)(2,1)S(1)}, u32[]{:S(2)}, u32[]{:S(2)}) async-start(bf16[32,8,640]{2,1,0:T(8,128)(2,1)} %bitcast.25), calls=%async_computation | async-start | bytes 655360 | tf_op jit(solution)/shard_map/all_to_all | solution.py:422
  17.8 7.9 %local_outputs.2 = (bf16[4096,512]{1,0:T(8,128)(2,1)}, f32[256,128]{1,0:T(8,128)}, f32[256,640]{1,0:T(8,128)}) custom-call(f32[256,128]{1,0:T(8,128)} %get-tuple-element.28.gates_ref, bf16[4096,256]{1,0:T(8,128)(2,1)} %bitcast.11, bf16[4096,256]{1,0:T(8,128)(2,1)} %bitcast.23, bf16[4096,512]{1,0:T(8,128)(2,1)} %bitcast.20), custom_call_target="tpu_custom_call" | custom-call | tf_op jit(solution)/shard_map/local_outputs/pallas_call | solution.py:271
  25.7 2.2 %all-to-all-done = bf16[32,8,640]{2,1,0:T(8,128)(2,1)S(1)} async-done(((bf16[32,8,640]{2,1,0:T(8,128)(2,1)}), bf16[32,8,640]{2,1,0:T(8,128)(2,1)S(1)}, u32[]{:S(2)}, u32[]{:S(2)}) %all-to-all-start) | async-done | bytes 327712 | tf_op jit(solution)/shard_map/all_to_all | solution.py:422
  28.0 1.6 %prefix_states.1 = bf16[256,640]{1,0:T(8,128)(2,1)} custom-call(bf16[256,640]{1,0:T(8,128)(2,1)S(1)} %bitcast.17), custom_call_target="tpu_custom_call" | custom-call | tf_op jit(solution)/shard_map/prefix_states/pallas_call | solution.py:212
  29.6 7.2 %all-to-all-start.1 = ((bf16[32,8,640]{2,1,0:T(8,128)(2,1)}), bf16[32,8,640]{2,1,0:T(8,128)(2,1)S(1)}, u32[]{:S(2)}, u32[]{:S(2)}) async-start(bf16[32,8,640]{2,1,0:T(8,128)(2,1)} %bitcast.9), calls=%async_computation.1 | async-start | bytes 655360 | tf_op jit(solution)/shard_map/all_to_all | solution.py:422
  36.8 0.0 copy-start.1
  36.8 0.0 copy-start.2
  36.8 8.4 %local_outputs.3 = (bf16[4096,512]{1,0:T(8,128)(2,1)}, f32[256,128]{1,0:T(8,128)}, f32[256,640]{1,0:T(8,128)}) custom-call(f32[256,128]{1,0:T(8,128)} %get-tuple-element.28.gates_ref, bf16[4096,256]{1,0:T(8,128)(2,1)} %bitcast.12, bf16[4096,256]{1,0:T(8,128)(2,1)} %bitcast.24, ...), custom_call_target="tpu_custom_call", output_to_operand_aliasing={{0}: (4, {}), {1}: (5, {})} | custom-call | tf_op jit(solution)/shard_map/local_outputs/pallas_call | solution.py:271
  45.2 1.5 %all-to-all-done.1 = bf16[32,8,640]{2,1,0:T(8,128)(2,1)S(1)} async-done(((bf16[32,8,640]{2,1,0:T(8,128)(2,1)}), bf16[32,8,640]{2,1,0:T(8,128)(2,1)S(1)}, u32[]{:S(2)}, u32[]{:S(2)}) %all-to-all-start.1) | async-done | bytes 327712 | tf_op jit(solution)/shard_map/all_to_all | solution.py:422
  46.7 0.0 copy-done.1
  46.7 0.0 copy-done.2
  46.7 0.0 copy-start
  46.7 2.2 %copy-done = bf16[4096,512]{1,0:T(8,128)(2,1)S(1)} copy-done((bf16[4096,512]{1,0:T(8,128)(2,1)S(1)}, bf16[4096,512]{1,0:T(8,128)(2,1)}, u32[]{:S(2)}) %copy-start) | copy-done | bytes 4194328
  48.9 0.0 copy-start.3
  48.9 0.9 copy-done.3
  49.8 2.3 %finish.3 = (bf16[512,512]{1,0:T(8,128)(2,1)S(1)}, bf16[512,512]{1,0:T(8,128)(2,1)S(1)}) custom-call(s32[1]{0:T(128)} %bitcast.place_ref, bf16[4096,256]{1,0:T(8,128)(2,1)S(1)} %bitcast.13, bf16[4096,512]{1,0:T(8,128)(2,1)S(1)} %copy-done, f32[256,128]{1,0:T(8,128)S(1)} %copy-done.2, f32[256,128]{1,0:T(8,128)S(1)} %copy-done.3, bf16[256,640]{1,0:T(8,128)(2,1)S(1)} %bitcast.15), custom_call_target="tpu_custom_call" | custom-call | flops 335544320 | bytes 2621440 | tf_op jit(solution)/shard_map/finish/pallas_call | solution.py:359
  52.1 0.0 copy-start.4
  52.1 7.2 %collective-permute-start.2 = (bf16[512,512]{1,0:T(8,128)(2,1)S(1)}, bf16[512,512]{1,0:T(8,128)(2,1)S(1)}, u32[]{:S(2)}, u32[]{:S(2)}) collective-permute-start(bf16[512,512]{1,0:T(8,128)(2,1)S(1)} %get-tuple-element.46), channel_id=1, source_target_pairs={{0,3},{1,4},{2,5},{3,6},{4,7},{5,0},{6,1},{7,2},{8,11},{9,12},{10,... | collective-permute-start | bytes 1572872 | tf_op jit(solution)/shard_map/ppermute | solution.py:447
  59.3 0.2 collective-permute-start.3
  59.6 6.9 %finish.2 = (bf16[512,512]{1,0:T(8,128)(2,1)S(1)}, bf16[512,512]{1,0:T(8,128)(2,1)S(1)}, bf16[512,512]{1,0:T(8,128)(2,1)S(1)}, bf16[512,512]{1,0:T(8,128)(2,1)S(...) custom-call(s32[1]{0:T(128)} %bitcast.place_ref, bf16[4096,256]{1,0:T(8,128)(2,1)S(1)} %bitcast.14, ...), custom_call_target="tpu_custom_call" | custom-call | flops 1006632960 | bytes 7864320 | tf_op jit(solution)/shard_map/finish/pallas_call | solution.py:359
  66.5 0.6 collective-permute-start
  67.2 0.7 collective-permute-start.1
  67.8 2.1 %collective-permute-start.4 = (bf16[512,512]{1,0:T(8,128)(2,1)S(1)}, bf16[512,512]{1,0:T(8,128)(2,1)S(1)}, u32[]{:S(2)}, u32[]{:S(2)}) collective-permute-start(bf16[512,512]{1,0:T(8,128)(2,1)S(1)} %get-tuple-element.48), channel_id=1, source_target_pairs={{0,5},{1,6},{2,7},{3,0},{4,1},{5,2},{6,3},{7,4},{8,13},{9,14},{10,... | collective-permute-start | bytes 1572872 | tf_op jit(solution)/shard_map/ppermute | solution.py:447
  69.9 13.6 %collective-permute-done.2.refs_3_ = bf16[512,512]{1,0:T(8,128)(2,1)S(1)} collective-permute-done((bf16[512,512]{1,0:T(8,128)(2,1)S(1)}, bf16[512,512]{1,0:T(8,128)(2,1)S(1)}, u32[]{:S(2)}, u32[]{:S(2)}) %collective-permute-start.2) | collective-permute-done | bytes 524320 | tf_op jit(solution)/shard_map/ppermute | solution.py:447
  83.5 0.0 collective-permute-start.5
  83.5 0.0 collective-permute-done.3.refs_4_
  83.5 0.3 collective-permute-start.6
  83.7 9.9 %collective-permute-done.refs_1_ = bf16[512,512]{1,0:T(8,128)(2,1)S(1)} collective-permute-done((bf16[512,512]{1,0:T(8,128)(2,1)S(1)}, bf16[512,512]{1,0:T(8,128)(2,1)S(1)}, u32[]{:S(2)}, u32[]{:S(2)}) %collective-permute-start) | collective-permute-done | bytes 524320 | tf_op jit(solution)/shard_map/ppermute | solution.py:447
  93.7 11.3 %collective-permute-done.1.refs_2_ = bf16[512,512]{1,0:T(8,128)(2,1)S(1)} collective-permute-done((bf16[512,512]{1,0:T(8,128)(2,1)S(1)}, bf16[512,512]{1,0:T(8,128)(2,1)S(1)}, u32[]{:S(2)}, u32[]{:S(2)}) %collective-permute-start.1) | collective-permute-done | bytes 524320 | tf_op jit(solution)/shard_map/ppermute | solution.py:447
  105.0 0.5 collective-permute-done.4.refs_5_
  105.4 0.0 collective-permute-done.5.refs_6_
  105.4 0.1 collective-permute-done.6.refs_7_
  105.6 0.0 copy-done.4
  105.6 3.5 %norm.1 = bf16[512,4096]{1,0:T(8,128)(2,1)} custom-call(s32[1]{0:T(128)} %bitcast.place_ref, f32[1,4096]{1,0:T(1,128)S(1)} %bitcast.18, bf16[512,512]{1,0:T(8,128)(2,1)S(1)} %get-tuple-element.43.refs_0_, bf16[512,512]{1,0:T(8,128)(2,1)S(1)} %collective-permute-done.refs_1_, bf16[512,512]{1,0:T(8,128)(2,1)S(1)} %collective-permute-done.1.refs_2_, ...), custom_call_target="tpu_custom_call" | custom-call | tf_op jit(solution)/shard_map/norm/pallas_call | solution.py:404
Async XLA Ops:
  5.8 22.2 %all-to-all-start = ((bf16[32,8,640]{2,1,0:T(8,128)(2,1)}), bf16[32,8,640]{2,1,0:T(8,128)(2,1)S(1)}, u32[]{:S(2)}, u32[]{:S(2)}) async-start(bf16[32,8,640]{2,1,0:T(8,128)(2,1)} %bitcast.25), calls=%async_computation | async-start | bytes 655360 | tf_op jit(solution)/shard_map/all_to_all | solution.py:422
  29.6 17.2 %all-to-all-start.1 = ((bf16[32,8,640]{2,1,0:T(8,128)(2,1)}), bf16[32,8,640]{2,1,0:T(8,128)(2,1)S(1)}, u32[]{:S(2)}, u32[]{:S(2)}) async-start(bf16[32,8,640]{2,1,0:T(8,128)(2,1)} %bitcast.9), calls=%async_computation.1 | async-start | bytes 655360 | tf_op jit(solution)/shard_map/all_to_all | solution.py:422
  36.8 9.9 %copy-start.1 = (bf16[4096,1,256]{2,0,1:T(8,128)(2,1)S(1)}, bf16[4096,1,256]{2,0,1:T(8,128)(2,1)}, u32[]{:S(2)}) copy-start(bf16[4096,1,256]{2,0,1:T(8,128)(2,1)} %param.6) | copy-start | bytes 6291460
  36.8 9.9 %copy-start.2 = (f32[256,128]{1,0:T(8,128)S(1)}, f32[256,128]{1,0:T(8,128)}, u32[]{:S(2)}) copy-start(f32[256,128]{1,0:T(8,128)} %get-tuple-element.28.gates_ref) | copy-start | bytes 393220
  46.7 2.2 %copy-start = (bf16[4096,512]{1,0:T(8,128)(2,1)S(1)}, bf16[4096,512]{1,0:T(8,128)(2,1)}, u32[]{:S(2)}) copy-start(bf16[4096,512]{1,0:T(8,128)(2,1)} %get-tuple-element.40.numer_hbm) | copy-start | bytes 12582916
  48.9 0.9 copy-start.3
  52.1 53.4 %copy-start.4 = (f32[4096]{0:T(1024)S(1)}, f32[4096]{0:T(1024)}, u32[]{:S(2)}) copy-start(f32[4096]{0:T(1024)} %param.11) | copy-start | bytes 49156
  52.1 31.3 %collective-permute-start.2 = (bf16[512,512]{1,0:T(8,128)(2,1)S(1)}, bf16[512,512]{1,0:T(8,128)(2,1)S(1)}, u32[]{:S(2)}, u32[]{:S(2)}) collective-permute-start(bf16[512,512]{1,0:T(8,128)(2,1)S(1)} %get-tuple-element.46), channel_id=1, source_target_pairs={{0,3},{1,4},{2,5},{3,6},{4,7},{5,0},{6,1},{7,2},{8,11},{9,12},{10,... | collective-permute-start | bytes 1572872 | tf_op jit(solution)/shard_map/ppermute | solution.py:447
  59.3 24.2 %collective-permute-start.3 = (bf16[512,512]{1,0:T(8,128)(2,1)S(1)}, bf16[512,512]{1,0:T(8,128)(2,1)S(1)}, u32[]{:S(2)}, u32[]{:S(2)}) collective-permute-start(bf16[512,512]{1,0:T(8,128)(2,1)S(1)} %get-tuple-element.47), channel_id=1, source_target_pairs={{0,4},{1,5},{2,6},{3,7},{4,0},{5,1},{6,2},{7,3},{8,12},{9,13},{10,... | collective-permute-start | bytes 1572872 | tf_op jit(solution)/shard_map/ppermute | solution.py:447
  66.5 27.2 %collective-permute-start = (bf16[512,512]{1,0:T(8,128)(2,1)S(1)}, bf16[512,512]{1,0:T(8,128)(2,1)S(1)}, u32[]{:S(2)}, u32[]{:S(2)}) collective-permute-start(bf16[512,512]{1,0:T(8,128)(2,1)S(1)} %get-tuple-element.44), channel_id=1, source_target_pairs={{0,1},{1,2},{2,3},{3,4},{4,5},{5,6},{6,7},{7,0},{8,9},{9,10},{10,1... | collective-permute-start | bytes 1572872 | tf_op jit(solution)/shard_map/ppermute | solution.py:447
  67.2 37.8 %collective-permute-start.1 = (bf16[512,512]{1,0:T(8,128)(2,1)S(1)}, bf16[512,512]{1,0:T(8,128)(2,1)S(1)}, u32[]{:S(2)}, u32[]{:S(2)}) collective-permute-start(bf16[512,512]{1,0:T(8,128)(2,1)S(1)} %get-tuple-element.45), channel_id=1, source_target_pairs={{0,2},{1,3},{2,4},{3,5},{4,6},{5,7},{6,0},{7,1},{8,10},{9,11},{10,... | collective-permute-start | bytes 1572872 | tf_op jit(solution)/shard_map/ppermute | solution.py:447
  67.8 37.6 %collective-permute-start.4 = (bf16[512,512]{1,0:T(8,128)(2,1)S(1)}, bf16[512,512]{1,0:T(8,128)(2,1)S(1)}, u32[]{:S(2)}, u32[]{:S(2)}) collective-permute-start(bf16[512,512]{1,0:T(8,128)(2,1)S(1)} %get-tuple-element.48), channel_id=1, source_target_pairs={{0,5},{1,6},{2,7},{3,0},{4,1},{5,2},{6,3},{7,4},{8,13},{9,14},{10,... | collective-permute-start | bytes 1572872 | tf_op jit(solution)/shard_map/ppermute | solution.py:447
  83.5 22.0 %collective-permute-start.5 = (bf16[512,512]{1,0:T(8,128)(2,1)S(1)}, bf16[512,512]{1,0:T(8,128)(2,1)S(1)}, u32[]{:S(2)}, u32[]{:S(2)}) collective-permute-start(bf16[512,512]{1,0:T(8,128)(2,1)S(1)} %get-tuple-element.49), channel_id=1, source_target_pairs={{0,6},{1,7},{2,0},{3,1},{4,2},{5,3},{6,4},{7,5},{8,14},{9,15},{10,... | collective-permute-start | bytes 1572872 | tf_op jit(solution)/shard_map/ppermute | solution.py:447
  83.5 22.1 %collective-permute-start.6 = (bf16[512,512]{1,0:T(8,128)(2,1)S(1)}, bf16[512,512]{1,0:T(8,128)(2,1)S(1)}, u32[]{:S(2)}, u32[]{:S(2)}) collective-permute-start(bf16[512,512]{1,0:T(8,128)(2,1)S(1)} %get-tuple-element.50), channel_id=1, source_target_pairs={{0,7},{1,0},{2,1},{3,2},{4,3},{5,4},{6,5},{7,6},{8,15},{9,8},{10,9... | collective-permute-start | bytes 1572872 | tf_op jit(solution)/shard_map/ppermute | solution.py:447

commit v3 on v2

--- a/solution.py
+++ b/solution.py
@@ -17,8 +17,8 @@
 VMEM_LIMIT = 60 * 1024 * 1024
 OUTPUTS_LIMIT = 60 * 1024 * 1024
 SMALL_LIMIT = 20 * 1024 * 1024
-FINISH_LIMIT = 24 * 1024 * 1024
-HOPS = ((4, 3), (5, 2, 6, 1, 7, 0))
+FINISH_LIMITS = (61 * 1024 * 1024, 61 * 1024 * 1024, 61 * 1024 * 1024,)
+HOPS = ((4,), (3, 5), (2, 6, 1, 7, 0))
 
 
 def dot(a, b):
@@ -295,10 +295,11 @@
 
 
 def finish(
-    place_ref, query_hbm, numer_hbm, gates_ref, stats_ref, packet_ref, *refs, hops, owners
+    place_ref, query_hbm, numer_hbm, gates_hbm, stats_hbm, packet_hbm, *refs, hops, owners
 ):
     outs = refs[: len(hops)]
-    query_ref, numer_ref, hidden_ref, in_sems, out_sems = refs[len(hops) :]
+    query_ref, numer_ref, gates_ref, stats_ref, packet_ref, hidden_ref, in_sems, all_sems, out_sems = refs[len(hops) :]
+    first = fetch([[(packet_hbm, packet_ref), (gates_hbm, gates_ref), (stats_hbm, stats_ref)]], all_sems)[0]
     rows = query_ref.shape[1]
     width = numer_ref.shape[2]
     scale = 1.0 / query_ref.shape[2] ** 0.5
@@ -310,6 +311,8 @@
             [(query_hbm.at[span, :], query_ref.at[number]), (numer_hbm.at[span, :], numer_ref.at[number])]
         )
     waits = fetch(blocks, in_sems)
+    for copy in first:
+        copy.wait()
     ends = packet_ref[0:16, width:].astype(F32)[0:1]
     entering = ends[:, 2:3] + ends[:, 3:4] + ends[:, 4:5]
     copies = []
@@ -348,27 +351,29 @@
         copy.wait()
 
 
-def run_finish(place, queries, numer, gates, stats, packet, owners, hops):
+def run_finish(place, queries, numer, gates, stats, packet, owners, hops, limit):
     tokens, depth = queries.shape
     width = numer.shape[1]
     rows = tokens // owners
     count = len(hops)
-    vmem = pl.BlockSpec(memory_space=pltpu.VMEM)
-    hbm = pl.BlockSpec(memory_space=pltpu.HBM)
     anywhere = pl.BlockSpec(memory_space=pl.ANY)
     return pl.pallas_call(
         functools.partial(finish, hops=hops, owners=owners),
-        in_specs=[pl.BlockSpec(memory_space=pltpu.SMEM), hbm, hbm, vmem, vmem, vmem],
+        in_specs=[pl.BlockSpec(memory_space=pltpu.SMEM)] + [anywhere] * 5,
         out_specs=[anywhere] * count,
         out_shape=[jax.ShapeDtypeStruct((rows, width), BF)] * count,
         scratch_shapes=[
             pltpu.VMEM((count, rows, depth), BF),
             pltpu.VMEM((count, rows, width), BF),
+            pltpu.VMEM(gates.shape, F32),
+            pltpu.VMEM(stats.shape, F32),
+            pltpu.VMEM(packet.shape, BF),
             pltpu.VMEM((count, rows, width), BF),
             pltpu.SemaphoreType.DMA((count, 2)),
+            pltpu.SemaphoreType.DMA((1, 3)),
             pltpu.SemaphoreType.DMA((count,)),
         ],
-        compiler_params=pltpu.CompilerParams(vmem_limit_bytes=FINISH_LIMIT),
+        compiler_params=pltpu.CompilerParams(vmem_limit_bytes=limit),
         cost_estimate=pl.CostEstimate(
             flops=2 * count * rows * depth * packet.shape[1],
             bytes_accessed=count * rows * (2 * depth + 4 * width),
@@ -440,8 +445,8 @@
     numer, stats, _ = run_local_outputs(gates, queries, keys, values, 1, before)
     parts = [None] * owners
     place = mine
-    for hops in HOPS:
-        group = run_finish(place, queries, numer, gates, stats, entering, owners, hops)
+    for hops, limit in zip(HOPS, FINISH_LIMITS):
+        group = run_finish(place, queries, numer, gates, stats, entering, owners, hops, limit)
         for hop, hidden in zip(hops, group):
             if hop:
                 hidden = lax.ppermute(hidden, "head", [(i, (i + hop) % owners) for i in range(owners)])

time: 110 us -> 106 us (0.964)
  waiting for transfers between devices: 39.1 us -> 25 us
  Pallas kernels: 36.5 us -> 42.7 us
  starting transfers between devices: 30.3 us -> 34.9 us
  local copies, waits for them, and re-layouts: 3.11 us -> 1.78 us
    ppermute x7, waiting for transfers between devices: 35.4 us -> 21.1 us  [shards(): lax.ppermute(hidden, 'head', [(i, (i + hop) % owners) for i in range(owne...]
    pallas_call x2 -> x3, Pallas kernels: 9.24 us -> 15.6 us  [run_finish(): pl.pallas_call(functools.partial(finish, hops=hops, owners=owners), in_sp...]
    ppermute x7, starting transfers between devices: 11.1 us -> 15.6 us  [shards(): lax.ppermute(hidden, 'head', [(i, (i + hop) % owners) for i in range(owne...]
    unnamed x10 -> x6, local copies, waits for them, and re-layouts: 3.11 us -> 1.78 us
  transfers between devices with their start and end apart: 9 -> 9, of which waited for: 7 -> 5; matrix products, arithmetic and copies ran while one was open for 0% -> 0% of each run, Pallas kernels for 21% -> 27%
where the time goes in v3:
time: 106 us; the launch traced here: 104 us
  Pallas kernels  42.7 us (40%)
  starting transfers between devices  34.9 us (33%)
  waiting for transfers between devices  25 us (24%)
  local copies, waits for them, and re-layouts  1.78 us (2%)
    ppermute x7, waiting for transfers between devices, shards(): lax.ppermute(hidden, 'head', [(i, (i + hop) % owners) for i in range(owne...  21.1 us
    all_to_all x2, starting transfers between devices, swap_slices(): return lax.all_to_all(cut, 'seq', 0, 0, tiled=True).reshape(rows, wide)  19.3 us
    pallas_call x2, Pallas kernels, run_local_outputs(): pl.pallas_call(local_outputs, grid=(steps,), in_specs=[pl.BlockSpec((bloc...  16.2 us
    ppermute x7, starting transfers between devices, shards(): lax.ppermute(hidden, 'head', [(i, (i + hop) % owners) for i in range(owne...  15.6 us
    pallas_call x3, Pallas kernels, run_finish(): pl.pallas_call(functools.partial(finish, hops=hops, owners=owners), in_sp...  15.6 us
    pallas_call x1, Pallas kernels, run_local_state(): pl.pallas_call(local_state, in_specs=[vmem, vmem, hbm, hbm], out_specs=[v...  5.77 us
    all_to_all x2, waiting for transfers between devices, swap_slices(): return lax.all_to_all(cut, 'seq', 0, 0, tiled=True).reshape(rows, wide)  3.86 us
    pallas_call x1, Pallas kernels, run_norm(): pl.pallas_call(norm, grid_spec=pltpu.PrefetchScalarGridSpec(num_scalar_pr...  3.53 us
  transfers between devices with their start and end apart: 9, of which 5 were waited for; matrix products, arithmetic and copies ran while one was open for 0% of the time, Pallas kernels for 27%

profile of v3, /device:TPU:1, one launch (start us, length us, event | category | flops | bytes accessed | tf_op | source)
XLA Modules:
  0.0 104.5 jit_solution(11267371324863228174)
XLA Ops:
  0.0 5.8 %local_state.1 = (bf16[256,640]{1,0:T(8,128)(2,1)}, f32[256,128]{1,0:T(8,128)}) custom-call(f32[32,128]{1,0:T(8,128)} %bitcast.28, f32[32,128]{1,0:T(8,128)} %bitcast.29, bf16[4096,256]{1,0:T(8,128)(2,1)} %bitcast.21, bf16[4096,512]{1,0:T(8,128)(2,1)} %bitcast.18), custom_call_target="tpu_custom_call" | custom-call | tf_op jit(solution)/shard_map/local_state/pallas_call | solution.py:161
  5.8 12.0 %all-to-all-start = ((bf16[32,8,640]{2,1,0:T(8,128)(2,1)}), bf16[32,8,640]{2,1,0:T(8,128)(2,1)S(1)}, u32[]{:S(2)}, u32[]{:S(2)}) async-start(bf16[32,8,640]{2,1,0:T(8,128)(2,1)} %bitcast.27), calls=%async_computation | async-start | bytes 655360 | tf_op jit(solution)/shard_map/all_to_all | solution.py:427
  17.8 7.9 %local_outputs.2 = (bf16[4096,512]{1,0:T(8,128)(2,1)}, f32[256,128]{1,0:T(8,128)}, f32[256,640]{1,0:T(8,128)}) custom-call(f32[256,128]{1,0:T(8,128)} %get-tuple-element.27.gates_ref.gates_hbm, bf16[4096,256]{1,0:T(8,128)(2,1)} %bitcast.13, bf16[4096,256]{1,0:T(8,128)(2,1)} %bitcast.22, bf16[4096,512]{1,0:T(8,128)(2,1)} %bitcast.19), custom_call_target="tpu_custom_call" | custom-call | tf_op jit(solution)/shard_map/local_outputs/pallas_call | solution.py:271
  25.7 2.2 %all-to-all-done = bf16[32,8,640]{2,1,0:T(8,128)(2,1)S(1)} async-done(((bf16[32,8,640]{2,1,0:T(8,128)(2,1)}), bf16[32,8,640]{2,1,0:T(8,128)(2,1)S(1)}, u32[]{:S(2)}, u32[]{:S(2)}) %all-to-all-start) | async-done | bytes 327712 | tf_op jit(solution)/shard_map/all_to_all | solution.py:427
  28.0 1.6 %prefix_states.1 = bf16[256,640]{1,0:T(8,128)(2,1)} custom-call(bf16[256,640]{1,0:T(8,128)(2,1)S(1)} %bitcast.11), custom_call_target="tpu_custom_call" | custom-call | tf_op jit(solution)/shard_map/prefix_states/pallas_call | solution.py:212
  29.6 7.2 %all-to-all-start.1 = ((bf16[32,8,640]{2,1,0:T(8,128)(2,1)}), bf16[32,8,640]{2,1,0:T(8,128)(2,1)S(1)}, u32[]{:S(2)}, u32[]{:S(2)}) async-start(bf16[32,8,640]{2,1,0:T(8,128)(2,1)} %bitcast.9), calls=%async_computation.1 | async-start | bytes 655360 | tf_op jit(solution)/shard_map/all_to_all | solution.py:427
  36.8 8.3 %local_outputs.3 = (bf16[4096,512]{1,0:T(8,128)(2,1)}, f32[256,128]{1,0:T(8,128)}, f32[256,640]{1,0:T(8,128)}) custom-call(f32[256,128]{1,0:T(8,128)} %get-tuple-element.27.gates_ref.gates_hbm, bf16[4096,256]{1,0:T(8,128)(2,1)} %bitcast.14, bf16[4096,256]{1,0:T(8,128)(2,1)} %bitcast.23, ...), custom_call_target="tpu_custom_call", output_to_operand_aliasing={{0}: (4, {}), {1}: (5, {})} | custom-call | tf_op jit(solution)/shard_map/local_outputs/pallas_call | solution.py:271
  45.1 1.6 %all-to-all-done.1 = bf16[32,8,640]{2,1,0:T(8,128)(2,1)S(1)} async-done(((bf16[32,8,640]{2,1,0:T(8,128)(2,1)}), bf16[32,8,640]{2,1,0:T(8,128)(2,1)S(1)}, u32[]{:S(2)}, u32[]{:S(2)}) %all-to-all-start.1) | async-done | bytes 327712 | tf_op jit(solution)/shard_map/all_to_all | solution.py:427
  46.7 0.0 copy-start.2
  46.8 0.7 copy-done.2
  47.5 3.1 %finish.5 = bf16[512,512]{1,0:T(8,128)(2,1)} custom-call(s32[1]{0:T(128)} %bitcast.place_ref, bf16[4096,256]{1,0:T(8,128)(2,1)} %bitcast.15, bf16[4096,512]{1,0:T(8,128)(2,1)} %get-tuple-element.39.numer_hbm, f32[256,128]{1,0:T(8,128)} %get-tuple-element.27.gates_ref.gates_hbm, f32[256,128]{1,0:T(8,128)} %get-tuple-element.40.stats_hbm, ...), custom_call_target="tpu_custom_call" | custom-call | flops 167772160 | bytes 1310720 | tf_op jit(solution)/shard_map/finish/pallas_call | solution.py:360
  50.6 2.8 %collective-permute-start.3 = (bf16[512,512]{1,0:T(8,128)(2,1)}, bf16[512,512]{1,0:T(8,128)(2,1)S(1)}, u32[]{:S(2)}, u32[]{:S(2)}) collective-permute-start(bf16[512,512]{1,0:T(8,128)(2,1)} %finish.5), channel_id=1, source_target_pairs={{0,4},{1,5},{2,6},{3,7},{4,0},{5,1},{6,2},{7,3},{8,12},{9,13},{10,... | collective-permute-start | bytes 1572872 | tf_op jit(solution)/shard_map/ppermute | solution.py:452
  53.4 4.3 %finish.4 = (bf16[512,512]{1,0:T(8,128)(2,1)}, bf16[512,512]{1,0:T(8,128)(2,1)}) custom-call(s32[1]{0:T(128)} %bitcast.place_ref, bf16[4096,256]{1,0:T(8,128)(2,1)} %bitcast.16, bf16[4096,512]{1,0:T(8,128)(2,1)} %get-tuple-element.39.numer_hbm, f32[256,128]{1,0:T(8,128)} %get-tuple-element.27.gates_ref.gates_hbm, f32[256,128]{1,0:T(8,128)} %get-tuple-element.40.stats_hbm, ...), custom_call_target="tpu_custom_call" | custom-call | flops 335544320 | bytes 2621440 | tf_op jit(solution)/shard_map/finish/pallas_call | solution.py:360
  57.7 0.0 copy-start.1
  57.8 5.1 %collective-permute-start.2 = (bf16[512,512]{1,0:T(8,128)(2,1)}, bf16[512,512]{1,0:T(8,128)(2,1)S(1)}, u32[]{:S(2)}, u32[]{:S(2)}) collective-permute-start(bf16[512,512]{1,0:T(8,128)(2,1)} %get-tuple-element.45), channel_id=1, source_target_pairs={{0,3},{1,4},{2,5},{3,6},{4,7},{5,0},{6,1},{7,2},{8,11},{9,12},{10,... | collective-permute-start | bytes 1572872 | tf_op jit(solution)/shard_map/ppermute | solution.py:452
  62.9 0.7 collective-permute-start.4
  63.6 8.2 %finish.3 = (bf16[512,512]{1,0:T(8,128)(2,1)}, bf16[512,512]{1,0:T(8,128)(2,1)}, bf16[512,512]{1,0:T(8,128)(2,1)}, bf16[512,512]{1,0:T(8,128)(2,1)}, bf16[512,512]{1,0:T(8,128)(2,1)}) custom-call(s32[1]{0:T(128)} %bitcast.place_ref, bf16[4096,256]{1,0:T(8,128)(2,1)} %bitcast.17, bf16[4096,512]{1,0:T(8,128)(2,1)} %get-tuple-element.39.numer_hbm, ...), custom_call_target="tpu_custom_call" | custom-call | flops 838860800 | bytes 6553600 | tf_op jit(solution)/shard_map/finish/pallas_call | solution.py:360
  71.8 2.6 %collective-permute-start = (bf16[512,512]{1,0:T(8,128)(2,1)}, bf16[512,512]{1,0:T(8,128)(2,1)S(1)}, u32[]{:S(2)}, u32[]{:S(2)}) collective-permute-start(bf16[512,512]{1,0:T(8,128)(2,1)} %get-tuple-element.43), channel_id=1, source_target_pairs={{0,1},{1,2},{2,3},{3,4},{4,5},{5,6},{6,7},{7,0},{8,9},{9,10},{10,1... | collective-permute-start | bytes 1572872 | tf_op jit(solution)/shard_map/ppermute | solution.py:452
  74.4 0.0 collective-permute-start.1
  74.4 0.0 collective-permute-done.3.refs_4_
  74.4 2.7 %collective-permute-start.5 = (bf16[512,512]{1,0:T(8,128)(2,1)}, bf16[512,512]{1,0:T(8,128)(2,1)S(1)}, u32[]{:S(2)}, u32[]{:S(2)}) collective-permute-start(bf16[512,512]{1,0:T(8,128)(2,1)} %get-tuple-element.47), channel_id=1, source_target_pairs={{0,6},{1,7},{2,0},{3,1},{4,2},{5,3},{6,4},{7,5},{8,14},{9,15},{10,... | collective-permute-start | bytes 1572872 | tf_op jit(solution)/shard_map/ppermute | solution.py:452
  77.1 0.0 collective-permute-done.2.refs_3_
  77.1 1.7 %collective-permute-start.6 = (bf16[512,512]{1,0:T(8,128)(2,1)}, bf16[512,512]{1,0:T(8,128)(2,1)S(1)}, u32[]{:S(2)}, u32[]{:S(2)}) collective-permute-start(bf16[512,512]{1,0:T(8,128)(2,1)} %get-tuple-element.48), channel_id=1, source_target_pairs={{0,7},{1,0},{2,1},{3,2},{4,3},{5,4},{6,5},{7,6},{8,15},{9,8},{10,9... | collective-permute-start | bytes 1572872 | tf_op jit(solution)/shard_map/ppermute | solution.py:452
  78.8 9.0 %collective-permute-done.4.refs_5_ = bf16[512,512]{1,0:T(8,128)(2,1)S(1)} collective-permute-done((bf16[512,512]{1,0:T(8,128)(2,1)}, bf16[512,512]{1,0:T(8,128)(2,1)S(1)}, u32[]{:S(2)}, u32[]{:S(2)}) %collective-permute-start.4) | collective-permute-done | bytes 524320 | tf_op jit(solution)/shard_map/ppermute | solution.py:452
  87.7 0.0 collective-permute-done.refs_1_
  87.7 12.0 %collective-permute-done.1.refs_2_ = bf16[512,512]{1,0:T(8,128)(2,1)S(1)} collective-permute-done((bf16[512,512]{1,0:T(8,128)(2,1)}, bf16[512,512]{1,0:T(8,128)(2,1)S(1)}, u32[]{:S(2)}, u32[]{:S(2)}) %collective-permute-start.1) | collective-permute-done | bytes 524320 | tf_op jit(solution)/shard_map/ppermute | solution.py:452
  99.8 0.0 collective-permute-done.5.refs_6_
  99.8 0.1 collective-permute-done.6.refs_7_
  99.9 0.0 copy-done.1
  99.9 0.0 copy-start
  99.9 1.0 copy-done
  100.9 3.5 %norm.1 = bf16[512,4096]{1,0:T(8,128)(2,1)} custom-call(s32[1]{0:T(128)} %bitcast.place_ref, f32[1,4096]{1,0:T(1,128)S(1)} %bitcast.12, bf16[512,512]{1,0:T(8,128)(2,1)S(1)} %copy-done, bf16[512,512]{1,0:T(8,128)(2,1)S(1)} %collective-permute-done.refs_1_, bf16[512,512]{1,0:T(8,128)(2,1)S(1)} %collective-permute-done.1.refs_2_, ...), custom_call_target="tpu_custom_call" | custom-call | tf_op jit(solution)/shard_map/norm/pallas_call | solution.py:409
Async XLA Ops:
  5.8 22.2 %all-to-all-start = ((bf16[32,8,640]{2,1,0:T(8,128)(2,1)}), bf16[32,8,640]{2,1,0:T(8,128)(2,1)S(1)}, u32[]{:S(2)}, u32[]{:S(2)}) async-start(bf16[32,8,640]{2,1,0:T(8,128)(2,1)} %bitcast.27), calls=%async_computation | async-start | bytes 655360 | tf_op jit(solution)/shard_map/all_to_all | solution.py:427
  29.6 17.2 %all-to-all-start.1 = ((bf16[32,8,640]{2,1,0:T(8,128)(2,1)}), bf16[32,8,640]{2,1,0:T(8,128)(2,1)S(1)}, u32[]{:S(2)}, u32[]{:S(2)}) async-start(bf16[32,8,640]{2,1,0:T(8,128)(2,1)} %bitcast.9), calls=%async_computation.1 | async-start | bytes 655360 | tf_op jit(solution)/shard_map/all_to_all | solution.py:427
  46.7 0.7 copy-start.2
  50.6 23.8 %collective-permute-start.3 = (bf16[512,512]{1,0:T(8,128)(2,1)}, bf16[512,512]{1,0:T(8,128)(2,1)S(1)}, u32[]{:S(2)}, u32[]{:S(2)}) collective-permute-start(bf16[512,512]{1,0:T(8,128)(2,1)} %finish.5), channel_id=1, source_target_pairs={{0,4},{1,5},{2,6},{3,7},{4,0},{5,1},{6,2},{7,3},{8,12},{9,13},{10,... | collective-permute-start | bytes 1572872 | tf_op jit(solution)/shard_map/ppermute | solution.py:452
  57.7 42.1 %copy-start.1 = (f32[4096]{0:T(1024)S(1)}, f32[4096]{0:T(1024)}, u32[]{:S(2)}) copy-start(f32[4096]{0:T(1024)} %param.11) | copy-start | bytes 49156
  57.8 19.4 %collective-permute-start.2 = (bf16[512,512]{1,0:T(8,128)(2,1)}, bf16[512,512]{1,0:T(8,128)(2,1)S(1)}, u32[]{:S(2)}, u32[]{:S(2)}) collective-permute-start(bf16[512,512]{1,0:T(8,128)(2,1)} %get-tuple-element.45), channel_id=1, source_target_pairs={{0,3},{1,4},{2,5},{3,6},{4,7},{5,0},{6,1},{7,2},{8,11},{9,12},{10,... | collective-permute-start | bytes 1572872 | tf_op jit(solution)/shard_map/ppermute | solution.py:452
  62.9 24.9 %collective-permute-start.4 = (bf16[512,512]{1,0:T(8,128)(2,1)}, bf16[512,512]{1,0:T(8,128)(2,1)S(1)}, u32[]{:S(2)}, u32[]{:S(2)}) collective-permute-start(bf16[512,512]{1,0:T(8,128)(2,1)} %get-tuple-element.46), channel_id=1, source_target_pairs={{0,5},{1,6},{2,7},{3,0},{4,1},{5,2},{6,3},{7,4},{8,13},{9,14},{10,... | collective-permute-start | bytes 1572872 | tf_op jit(solution)/shard_map/ppermute | solution.py:452
  71.8 15.9 %collective-permute-start = (bf16[512,512]{1,0:T(8,128)(2,1)}, bf16[512,512]{1,0:T(8,128)(2,1)S(1)}, u32[]{:S(2)}, u32[]{:S(2)}) collective-permute-start(bf16[512,512]{1,0:T(8,128)(2,1)} %get-tuple-element.43), channel_id=1, source_target_pairs={{0,1},{1,2},{2,3},{3,4},{4,5},{5,6},{6,7},{7,0},{8,9},{9,10},{10,1... | collective-permute-start | bytes 1572872 | tf_op jit(solution)/shard_map/ppermute | solution.py:452
  74.4 25.3 %collective-permute-start.1 = (bf16[512,512]{1,0:T(8,128)(2,1)}, bf16[512,512]{1,0:T(8,128)(2,1)S(1)}, u32[]{:S(2)}, u32[]{:S(2)}) collective-permute-start(bf16[512,512]{1,0:T(8,128)(2,1)} %get-tuple-element.44), channel_id=1, source_target_pairs={{0,2},{1,3},{2,4},{3,5},{4,6},{5,7},{6,0},{7,1},{8,10},{9,11},{10,... | collective-permute-start | bytes 1572872 | tf_op jit(solution)/shard_map/ppermute | solution.py:452
  74.4 25.3 %collective-permute-start.5 = (bf16[512,512]{1,0:T(8,128)(2,1)}, bf16[512,512]{1,0:T(8,128)(2,1)S(1)}, u32[]{:S(2)}, u32[]{:S(2)}) collective-permute-start(bf16[512,512]{1,0:T(8,128)(2,1)} %get-tuple-element.47), channel_id=1, source_target_pairs={{0,6},{1,7},{2,0},{3,1},{4,2},{5,3},{6,4},{7,5},{8,14},{9,15},{10,... | collective-permute-start | bytes 1572872 | tf_op jit(solution)/shard_map/ppermute | solution.py:452
  77.1 22.8 %collective-permute-start.6 = (bf16[512,512]{1,0:T(8,128)(2,1)}, bf16[512,512]{1,0:T(8,128)(2,1)S(1)}, u32[]{:S(2)}, u32[]{:S(2)}) collective-permute-start(bf16[512,512]{1,0:T(8,128)(2,1)} %get-tuple-element.48), channel_id=1, source_target_pairs={{0,7},{1,0},{2,1},{3,2},{4,3},{5,4},{6,5},{7,6},{8,15},{9,8},{10,9... | collective-permute-start | bytes 1572872 | tf_op jit(solution)/shard_map/ppermute | solution.py:452
  99.9 1.0 copy-start

commit v4 on v3

--- a/solution.py
+++ b/solution.py
@@ -404,7 +404,7 @@
 
 def run_norm(place, gain, parts):
     rows, width = parts[0].shape
-    block = 128
+    block = 256
     total = width * len(parts)
     return pl.pallas_call(
         norm,

time: 106 us -> 106 us (level)
  no operation moved by 1% of the time
where the time goes in v4:
time: 106 us; the launch traced here: 105 us
  Pallas kernels  42.9 us (40%)
  starting transfers between devices  34.9 us (33%)
  waiting for transfers between devices  25 us (24%)
  local copies, waits for them, and re-layouts  1.78 us (2%)
    ppermute x7, waiting for transfers between devices, shards(): lax.ppermute(hidden, 'head', [(i, (i + hop) % owners) for i in range(owne...  21.1 us
    all_to_all x2, starting transfers between devices, swap_slices(): return lax.all_to_all(cut, 'seq', 0, 0, tiled=True).reshape(rows, wide)  19.3 us
    pallas_call x2, Pallas kernels, run_local_outputs(): pl.pallas_call(local_outputs, grid=(steps,), in_specs=[pl.BlockSpec((bloc...  16.2 us
    ppermute x7, starting transfers between devices, shards(): lax.ppermute(hidden, 'head', [(i, (i + hop) % owners) for i in range(owne...  15.6 us
    pallas_call x3, Pallas kernels, run_finish(): pl.pallas_call(functools.partial(finish, hops=hops, owners=owners), in_sp...  15.6 us
    pallas_call x1, Pallas kernels, run_local_state(): pl.pallas_call(local_state, in_specs=[vmem, vmem, hbm, hbm], out_specs=[v...  5.77 us
    all_to_all x2, waiting for transfers between devices, swap_slices(): return lax.all_to_all(cut, 'seq', 0, 0, tiled=True).reshape(rows, wide)  3.86 us
    pallas_call x1, Pallas kernels, run_norm(): pl.pallas_call(norm, grid_spec=pltpu.PrefetchScalarGridSpec(num_scalar_pr...  3.67 us
  transfers between devices with their start and end apart: 9, of which 5 were waited for; matrix products, arithmetic and copies ran while one was open for 0% of the time, Pallas kernels for 27%

profile of v4, /device:TPU:1, one launch (start us, length us, event | category | flops | bytes accessed | tf_op | source)
XLA Modules:
  0.0 104.6 jit_solution(15310366656101937682)
XLA Ops:
  0.0 5.8 %local_state.1 = (bf16[256,640]{1,0:T(8,128)(2,1)}, f32[256,128]{1,0:T(8,128)}) custom-call(f32[32,128]{1,0:T(8,128)} %bitcast.28, f32[32,128]{1,0:T(8,128)} %bitcast.29, bf16[4096,256]{1,0:T(8,128)(2,1)} %bitcast.21, bf16[4096,512]{1,0:T(8,128)(2,1)} %bitcast.18), custom_call_target="tpu_custom_call" | custom-call | tf_op jit(solution)/shard_map/local_state/pallas_call | solution.py:161
  5.8 12.0 %all-to-all-start = ((bf16[32,8,640]{2,1,0:T(8,128)(2,1)}), bf16[32,8,640]{2,1,0:T(8,128)(2,1)S(1)}, u32[]{:S(2)}, u32[]{:S(2)}) async-start(bf16[32,8,640]{2,1,0:T(8,128)(2,1)} %bitcast.27), calls=%async_computation | async-start | bytes 655360 | tf_op jit(solution)/shard_map/all_to_all | solution.py:427
  17.8 7.9 %local_outputs.2 = (bf16[4096,512]{1,0:T(8,128)(2,1)}, f32[256,128]{1,0:T(8,128)}, f32[256,640]{1,0:T(8,128)}) custom-call(f32[256,128]{1,0:T(8,128)} %get-tuple-element.27.gates_ref.gates_hbm, bf16[4096,256]{1,0:T(8,128)(2,1)} %bitcast.13, bf16[4096,256]{1,0:T(8,128)(2,1)} %bitcast.22, bf16[4096,512]{1,0:T(8,128)(2,1)} %bitcast.19), custom_call_target="tpu_custom_call" | custom-call | tf_op jit(solution)/shard_map/local_outputs/pallas_call | solution.py:271
  25.7 2.2 %all-to-all-done = bf16[32,8,640]{2,1,0:T(8,128)(2,1)S(1)} async-done(((bf16[32,8,640]{2,1,0:T(8,128)(2,1)}), bf16[32,8,640]{2,1,0:T(8,128)(2,1)S(1)}, u32[]{:S(2)}, u32[]{:S(2)}) %all-to-all-start) | async-done | bytes 327712 | tf_op jit(solution)/shard_map/all_to_all | solution.py:427
  28.0 1.6 %prefix_states.1 = bf16[256,640]{1,0:T(8,128)(2,1)} custom-call(bf16[256,640]{1,0:T(8,128)(2,1)S(1)} %bitcast.11), custom_call_target="tpu_custom_call" | custom-call | tf_op jit(solution)/shard_map/prefix_states/pallas_call | solution.py:212
  29.6 7.2 %all-to-all-start.1 = ((bf16[32,8,640]{2,1,0:T(8,128)(2,1)}), bf16[32,8,640]{2,1,0:T(8,128)(2,1)S(1)}, u32[]{:S(2)}, u32[]{:S(2)}) async-start(bf16[32,8,640]{2,1,0:T(8,128)(2,1)} %bitcast.9), calls=%async_computation.1 | async-start | bytes 655360 | tf_op jit(solution)/shard_map/all_to_all | solution.py:427
  36.8 8.3 %local_outputs.3 = (bf16[4096,512]{1,0:T(8,128)(2,1)}, f32[256,128]{1,0:T(8,128)}, f32[256,640]{1,0:T(8,128)}) custom-call(f32[256,128]{1,0:T(8,128)} %get-tuple-element.27.gates_ref.gates_hbm, bf16[4096,256]{1,0:T(8,128)(2,1)} %bitcast.14, bf16[4096,256]{1,0:T(8,128)(2,1)} %bitcast.23, ...), custom_call_target="tpu_custom_call", output_to_operand_aliasing={{0}: (4, {}), {1}: (5, {})} | custom-call | tf_op jit(solution)/shard_map/local_outputs/pallas_call | solution.py:271
  45.1 1.6 %all-to-all-done.1 = bf16[32,8,640]{2,1,0:T(8,128)(2,1)S(1)} async-done(((bf16[32,8,640]{2,1,0:T(8,128)(2,1)}), bf16[32,8,640]{2,1,0:T(8,128)(2,1)S(1)}, u32[]{:S(2)}, u32[]{:S(2)}) %all-to-all-start.1) | async-done | bytes 327712 | tf_op jit(solution)/shard_map/all_to_all | solution.py:427
  46.7 0.0 copy-start.2
  46.8 0.7 copy-done.2
  47.5 3.1 %finish.5 = bf16[512,512]{1,0:T(8,128)(2,1)} custom-call(s32[1]{0:T(128)} %bitcast.place_ref, bf16[4096,256]{1,0:T(8,128)(2,1)} %bitcast.15, bf16[4096,512]{1,0:T(8,128)(2,1)} %get-tuple-element.39.numer_hbm, f32[256,128]{1,0:T(8,128)} %get-tuple-element.27.gates_ref.gates_hbm, f32[256,128]{1,0:T(8,128)} %get-tuple-element.40.stats_hbm, ...), custom_call_target="tpu_custom_call" | custom-call | flops 167772160 | bytes 1310720 | tf_op jit(solution)/shard_map/finish/pallas_call | solution.py:360
  50.6 2.8 %collective-permute-start.3 = (bf16[512,512]{1,0:T(8,128)(2,1)}, bf16[512,512]{1,0:T(8,128)(2,1)S(1)}, u32[]{:S(2)}, u32[]{:S(2)}) collective-permute-start(bf16[512,512]{1,0:T(8,128)(2,1)} %finish.5), channel_id=1, source_target_pairs={{0,4},{1,5},{2,6},{3,7},{4,0},{5,1},{6,2},{7,3},{8,12},{9,13},{10,... | collective-permute-start | bytes 1572872 | tf_op jit(solution)/shard_map/ppermute | solution.py:452
  53.4 4.3 %finish.4 = (bf16[512,512]{1,0:T(8,128)(2,1)}, bf16[512,512]{1,0:T(8,128)(2,1)}) custom-call(s32[1]{0:T(128)} %bitcast.place_ref, bf16[4096,256]{1,0:T(8,128)(2,1)} %bitcast.16, bf16[4096,512]{1,0:T(8,128)(2,1)} %get-tuple-element.39.numer_hbm, f32[256,128]{1,0:T(8,128)} %get-tuple-element.27.gates_ref.gates_hbm, f32[256,128]{1,0:T(8,128)} %get-tuple-element.40.stats_hbm, ...), custom_call_target="tpu_custom_call" | custom-call | flops 335544320 | bytes 2621440 | tf_op jit(solution)/shard_map/finish/pallas_call | solution.py:360
  57.7 0.0 copy-start.1
  57.8 5.1 %collective-permute-start.2 = (bf16[512,512]{1,0:T(8,128)(2,1)}, bf16[512,512]{1,0:T(8,128)(2,1)S(1)}, u32[]{:S(2)}, u32[]{:S(2)}) collective-permute-start(bf16[512,512]{1,0:T(8,128)(2,1)} %get-tuple-element.45), channel_id=1, source_target_pairs={{0,3},{1,4},{2,5},{3,6},{4,7},{5,0},{6,1},{7,2},{8,11},{9,12},{10,... | collective-permute-start | bytes 1572872 | tf_op jit(solution)/shard_map/ppermute | solution.py:452
  62.9 0.7 collective-permute-start.4
  63.6 8.2 %finish.3 = (bf16[512,512]{1,0:T(8,128)(2,1)}, bf16[512,512]{1,0:T(8,128)(2,1)}, bf16[512,512]{1,0:T(8,128)(2,1)}, bf16[512,512]{1,0:T(8,128)(2,1)}, bf16[512,512]{1,0:T(8,128)(2,1)}) custom-call(s32[1]{0:T(128)} %bitcast.place_ref, bf16[4096,256]{1,0:T(8,128)(2,1)} %bitcast.17, bf16[4096,512]{1,0:T(8,128)(2,1)} %get-tuple-element.39.numer_hbm, ...), custom_call_target="tpu_custom_call" | custom-call | flops 838860800 | bytes 6553600 | tf_op jit(solution)/shard_map/finish/pallas_call | solution.py:360
  71.8 2.6 %collective-permute-start = (bf16[512,512]{1,0:T(8,128)(2,1)}, bf16[512,512]{1,0:T(8,128)(2,1)S(1)}, u32[]{:S(2)}, u32[]{:S(2)}) collective-permute-start(bf16[512,512]{1,0:T(8,128)(2,1)} %get-tuple-element.43), channel_id=1, source_target_pairs={{0,1},{1,2},{2,3},{3,4},{4,5},{5,6},{6,7},{7,0},{8,9},{9,10},{10,1... | collective-permute-start | bytes 1572872 | tf_op jit(solution)/shard_map/ppermute | solution.py:452
  74.4 0.0 collective-permute-start.1
  74.4 0.0 collective-permute-done.3.refs_4_
  74.4 2.7 %collective-permute-start.5 = (bf16[512,512]{1,0:T(8,128)(2,1)}, bf16[512,512]{1,0:T(8,128)(2,1)S(1)}, u32[]{:S(2)}, u32[]{:S(2)}) collective-permute-start(bf16[512,512]{1,0:T(8,128)(2,1)} %get-tuple-element.47), channel_id=1, source_target_pairs={{0,6},{1,7},{2,0},{3,1},{4,2},{5,3},{6,4},{7,5},{8,14},{9,15},{10,... | collective-permute-start | bytes 1572872 | tf_op jit(solution)/shard_map/ppermute | solution.py:452
  77.1 0.0 collective-permute-done.2.refs_3_
  77.1 1.7 %collective-permute-start.6 = (bf16[512,512]{1,0:T(8,128)(2,1)}, bf16[512,512]{1,0:T(8,128)(2,1)S(1)}, u32[]{:S(2)}, u32[]{:S(2)}) collective-permute-start(bf16[512,512]{1,0:T(8,128)(2,1)} %get-tuple-element.48), channel_id=1, source_target_pairs={{0,7},{1,0},{2,1},{3,2},{4,3},{5,4},{6,5},{7,6},{8,15},{9,8},{10,9... | collective-permute-start | bytes 1572872 | tf_op jit(solution)/shard_map/ppermute | solution.py:452
  78.8 9.0 %collective-permute-done.4.refs_5_ = bf16[512,512]{1,0:T(8,128)(2,1)S(1)} collective-permute-done((bf16[512,512]{1,0:T(8,128)(2,1)}, bf16[512,512]{1,0:T(8,128)(2,1)S(1)}, u32[]{:S(2)}, u32[]{:S(2)}) %collective-permute-start.4) | collective-permute-done | bytes 524320 | tf_op jit(solution)/shard_map/ppermute | solution.py:452
  87.7 0.0 collective-permute-done.refs_1_
  87.7 12.0 %collective-permute-done.1.refs_2_ = bf16[512,512]{1,0:T(8,128)(2,1)S(1)} collective-permute-done((bf16[512,512]{1,0:T(8,128)(2,1)}, bf16[512,512]{1,0:T(8,128)(2,1)S(1)}, u32[]{:S(2)}, u32[]{:S(2)}) %collective-permute-start.1) | collective-permute-done | bytes 524320 | tf_op jit(solution)/shard_map/ppermute | solution.py:452
  99.8 0.0 collective-permute-done.5.refs_6_
  99.8 0.1 collective-permute-done.6.refs_7_
  99.9 0.0 copy-done.1
  99.9 0.0 copy-start
  99.9 1.0 copy-done
  100.9 3.7 %norm.1 = bf16[512,4096]{1,0:T(8,128)(2,1)} custom-call(s32[1]{0:T(128)} %bitcast.place_ref, f32[1,4096]{1,0:T(1,128)S(1)} %bitcast.12, bf16[512,512]{1,0:T(8,128)(2,1)S(1)} %copy-done, bf16[512,512]{1,0:T(8,128)(2,1)S(1)} %collective-permute-done.refs_1_, bf16[512,512]{1,0:T(8,128)(2,1)S(1)} %collective-permute-done.1.refs_2_, ...), custom_call_target="tpu_custom_call" | custom-call | tf_op jit(solution)/shard_map/norm/pallas_call | solution.py:409
Async XLA Ops:
  5.8 22.2 %all-to-all-start = ((bf16[32,8,640]{2,1,0:T(8,128)(2,1)}), bf16[32,8,640]{2,1,0:T(8,128)(2,1)S(1)}, u32[]{:S(2)}, u32[]{:S(2)}) async-start(bf16[32,8,640]{2,1,0:T(8,128)(2,1)} %bitcast.27), calls=%async_computation | async-start | bytes 655360 | tf_op jit(solution)/shard_map/all_to_all | solution.py:427
  29.6 17.2 %all-to-all-start.1 = ((bf16[32,8,640]{2,1,0:T(8,128)(2,1)}), bf16[32,8,640]{2,1,0:T(8,128)(2,1)S(1)}, u32[]{:S(2)}, u32[]{:S(2)}) async-start(bf16[32,8,640]{2,1,0:T(8,128)(2,1)} %bitcast.9), calls=%async_computation.1 | async-start | bytes 655360 | tf_op jit(solution)/shard_map/all_to_all | solution.py:427
  46.7 0.7 copy-start.2
  50.6 23.8 %collective-permute-start.3 = (bf16[512,512]{1,0:T(8,128)(2,1)}, bf16[512,512]{1,0:T(8,128)(2,1)S(1)}, u32[]{:S(2)}, u32[]{:S(2)}) collective-permute-start(bf16[512,512]{1,0:T(8,128)(2,1)} %finish.5), channel_id=1, source_target_pairs={{0,4},{1,5},{2,6},{3,7},{4,0},{5,1},{6,2},{7,3},{8,12},{9,13},{10,... | collective-permute-start | bytes 1572872 | tf_op jit(solution)/shard_map/ppermute | solution.py:452
  57.7 42.1 %copy-start.1 = (f32[4096]{0:T(1024)S(1)}, f32[4096]{0:T(1024)}, u32[]{:S(2)}) copy-start(f32[4096]{0:T(1024)} %param.11) | copy-start | bytes 49156
  57.8 19.4 %collective-permute-start.2 = (bf16[512,512]{1,0:T(8,128)(2,1)}, bf16[512,512]{1,0:T(8,128)(2,1)S(1)}, u32[]{:S(2)}, u32[]{:S(2)}) collective-permute-start(bf16[512,512]{1,0:T(8,128)(2,1)} %get-tuple-element.45), channel_id=1, source_target_pairs={{0,3},{1,4},{2,5},{3,6},{4,7},{5,0},{6,1},{7,2},{8,11},{9,12},{10,... | collective-permute-start | bytes 1572872 | tf_op jit(solution)/shard_map/ppermute | solution.py:452
  62.9 24.9 %collective-permute-start.4 = (bf16[512,512]{1,0:T(8,128)(2,1)}, bf16[512,512]{1,0:T(8,128)(2,1)S(1)}, u32[]{:S(2)}, u32[]{:S(2)}) collective-permute-start(bf16[512,512]{1,0:T(8,128)(2,1)} %get-tuple-element.46), channel_id=1, source_target_pairs={{0,5},{1,6},{2,7},{3,0},{4,1},{5,2},{6,3},{7,4},{8,13},{9,14},{10,... | collective-permute-start | bytes 1572872 | tf_op jit(solution)/shard_map/ppermute | solution.py:452
  71.8 15.9 %collective-permute-start = (bf16[512,512]{1,0:T(8,128)(2,1)}, bf16[512,512]{1,0:T(8,128)(2,1)S(1)}, u32[]{:S(2)}, u32[]{:S(2)}) collective-permute-start(bf16[512,512]{1,0:T(8,128)(2,1)} %get-tuple-element.43), channel_id=1, source_target_pairs={{0,1},{1,2},{2,3},{3,4},{4,5},{5,6},{6,7},{7,0},{8,9},{9,10},{10,1... | collective-permute-start | bytes 1572872 | tf_op jit(solution)/shard_map/ppermute | solution.py:452
  74.4 25.3 %collective-permute-start.1 = (bf16[512,512]{1,0:T(8,128)(2,1)}, bf16[512,512]{1,0:T(8,128)(2,1)S(1)}, u32[]{:S(2)}, u32[]{:S(2)}) collective-permute-start(bf16[512,512]{1,0:T(8,128)(2,1)} %get-tuple-element.44), channel_id=1, source_target_pairs={{0,2},{1,3},{2,4},{3,5},{4,6},{5,7},{6,0},{7,1},{8,10},{9,11},{10,... | collective-permute-start | bytes 1572872 | tf_op jit(solution)/shard_map/ppermute | solution.py:452
  74.4 25.3 %collective-permute-start.5 = (bf16[512,512]{1,0:T(8,128)(2,1)}, bf16[512,512]{1,0:T(8,128)(2,1)S(1)}, u32[]{:S(2)}, u32[]{:S(2)}) collective-permute-start(bf16[512,512]{1,0:T(8,128)(2,1)} %get-tuple-element.47), channel_id=1, source_target_pairs={{0,6},{1,7},{2,0},{3,1},{4,2},{5,3},{6,4},{7,5},{8,14},{9,15},{10,... | collective-permute-start | bytes 1572872 | tf_op jit(solution)/shard_map/ppermute | solution.py:452
  77.1 22.8 %collective-permute-start.6 = (bf16[512,512]{1,0:T(8,128)(2,1)}, bf16[512,512]{1,0:T(8,128)(2,1)S(1)}, u32[]{:S(2)}, u32[]{:S(2)}) collective-permute-start(bf16[512,512]{1,0:T(8,128)(2,1)} %get-tuple-element.48), channel_id=1, source_target_pairs={{0,7},{1,0},{2,1},{3,2},{4,3},{5,4},{6,5},{7,6},{8,15},{9,8},{10,9... | collective-permute-start | bytes 1572872 | tf_op jit(solution)/shard_map/ppermute | solution.py:452
  99.9 1.0 copy-start
